TPU v7x, 512 devices: a whole 4x4x16 slice. The times are simulated.
512 devices in a mesh: brick: 64 (over z, x), chan: 8 (over y, core).
Axes of the slice: x: 4, y: 4, z: 16, core: 2. Of those that a mesh axis runs over, the one named last changes fastest.
Arguments:
- features: bfloat16 [512, 96, 512], P(('brick', 'chan')), may hold values from -6 to 6
- occupancy: int32 [512, 512], P(('brick', 'chan')), may hold values from 0 to 1
- neighbors: int32 [512, 27], P(('brick', 'chan')), may hold values from -1 to 511, as said below
- weight: bfloat16 [27, 96, 96], replicated, may hold values from -0.125 to 0.125
- grad_output: bfloat16 [512, 96, 512], P(('brick', 'chan')), may hold values from -6 to 6
Outputs:
- output: bfloat16 [512, 96, 512], P(('brick', 'chan'))
- grad_features: bfloat16 [512, 96, 512], P(('brick', 'chan'))
- grad_weight: float32 [27, 96, 96], replicated
Inputs may be any that keep to these rules, and one draw needn't show every extreme that they name: `neighbors`: column 13 holds the brick's own index. Every other entry is -1 or a brick held by the same device or the one just below or above it along brick+chan (1 bricks a device, in order).
All inputs are finite; a program needn't handle non-finite values.
Results may differ from a plain program's by a relative error of at most 0.0055.
Values may be sent and summed in bfloat16 or wider, within the bound.
No kernel may reach another device: no remote copies, remote signals or barrier semaphores. Data moves between devices by JAX's collectives and lax.ppermute only.
A program may use at most 64 MiB of HBM per device.

v0:
```python
import jax
import jax.numpy as jnp
from jax import lax
from jax.sharding import PartitionSpec as P

OFFSETS = [(dx, dy, dz) for dx in (-1, 0, 1) for dy in (-1, 0, 1) for dz in (-1, 0, 1)]


def padded_2(cells, sides, width):
    for axis, dim in sides:
        count = lax.axis_size(axis)
        ends = count - 1
        head = lax.slice_in_dim(cells, 0, width, axis=dim)
        tail = lax.slice_in_dim(cells, cells.shape[dim] - width, cells.shape[dim], axis=dim)
        cells = jnp.concatenate(
            [
                lax.ppermute(tail, axis, [(i, (i + 1) % count) for i in range(ends)]),
                cells,
                lax.ppermute(head, axis, [((i + 1) % count, i) for i in range(ends)]),
            ],
            axis=dim,
        )
    return cells


def from_behind(block, axis, distance):
    devices = range(lax.axis_size(axis))
    route = [(i - distance, i) for i in devices if i - distance in devices]
    return lax.ppermute(block, axis, route)


def region(stride):
    if stride < 0:
        return (slice(7, 8), slice(0, 1))
    if stride > 0:
        return (slice(0, 1), slice(9, 10))
    return (slice(0, 8), slice(1, 9))


def assemble(source, lookup):
    number = lookup.shape[0]
    depth = source.shape[1]
    cubes = source.reshape(source.shape[0], depth, 8, 8, 8)
    padded = jnp.zeros((number, depth, 10, 10, 10), source.dtype)
    for offset_id, shift in enumerate(OFFSETS):
        src_x, dst_x = region(shift[0])
        src_y, dst_y = region(shift[1])
        src_z, dst_z = region(shift[2])
        slab = cubes[:, :, src_x, src_y, src_z]
        picked = jnp.take(slab, lookup[:, offset_id], axis=0)
        padded = padded.at[:, :, dst_x, dst_y, dst_z].set(picked)
    return padded


def disperse(grads, lookup, total):
    depth = grads.shape[1]
    buffer = jnp.zeros((total + 1, depth, 8, 8, 8), jnp.float32)
    for offset_id, shift in enumerate(OFFSETS):
        src_x, dst_x = region(shift[0])
        src_y, dst_y = region(shift[1])
        src_z, dst_z = region(shift[2])
        buffer = buffer.at[lookup[:, offset_id], :, src_x, src_y, src_z].add(
            grads[:, :, dst_x, dst_y, dst_z]
        )
    return buffer[:total]


def backward_cells(weight, cotan, count, depth):
    grad_padded = jnp.zeros((count, depth, 10, 10, 10), jnp.float32)
    for tap, shift in enumerate(OFFSETS):
        low_x, low_y, low_z = (shift[0] + 1, shift[1] + 1, shift[2] + 1)
        back = jnp.einsum("co,bov->bcv", weight[tap], cotan, preferred_element_type=jnp.float32)
        grad_padded = grad_padded.at[
            :, :, low_x : low_x + 8, low_y : low_y + 8, low_z : low_z + 8
        ].add(back.reshape(count, depth, 8, 8, 8))
    return grad_padded


def shards(features, occupancy, neighbors, weight, grad_output):
    bricks = features.shape[0]
    depth = features.shape[1]
    occ_float = occupancy.reshape(bricks, 1, 512).astype(jnp.float32)
    occ_half = occupancy.reshape(bricks, 1, 512).astype(jnp.bfloat16)
    masked = features * occ_half
    nearby = padded_2(masked, ((("brick", "chan"), 0),), bricks)
    position = lax.axis_index(("brick", "chan"))
    base_id = (position - 1) * bricks
    lookup = jnp.where(neighbors >= 0, neighbors - base_id, 3 * bricks)
    source = jnp.concatenate([nearby, jnp.zeros((1, depth, 512), jnp.bfloat16)], axis=0)
    padded = assemble(source, lookup)
    cotangent = grad_output * occ_half
    summed = jnp.zeros((bricks, depth, 512), jnp.float32)
    tap_grads = []
    for tap, shift in enumerate(OFFSETS):
        low_x, low_y, low_z = (shift[0] + 1, shift[1] + 1, shift[2] + 1)
        window = padded[:, :, low_x : low_x + 8, low_y : low_y + 8, low_z : low_z + 8].reshape(
            bricks, depth, 512
        )
        summed = summed + jnp.einsum(
            "co,bcv->bov", weight[tap], window, preferred_element_type=jnp.float32
        )
        tap_grads.append(
            jnp.einsum("bcv,bov->co", window, cotangent, preferred_element_type=jnp.float32)
        )
    output = (summed * occ_float).astype(jnp.bfloat16)
    grad_weight = lax.psum(jnp.stack(tap_grads, axis=0), ("brick", "chan"))
    grad_padded = backward_cells(weight, cotangent, bricks, depth)
    returned = disperse(grad_padded, lookup, 3 * bricks).reshape(3, bricks, depth, 512)
    from_upper = from_behind(returned[0].astype(jnp.bfloat16), ("brick", "chan"), -1).astype(
        jnp.float32
    )
    from_lower = from_behind(returned[2].astype(jnp.bfloat16), ("brick", "chan"), 1).astype(
        jnp.float32
    )
    grad_source = returned[1] + from_upper + from_lower
    grad_features = (grad_source * occ_float).astype(jnp.bfloat16)
    return (output, grad_features, grad_weight)


def solution(mesh):
    placed = (
        P(("brick", "chan"), None, None),
        P(("brick", "chan"), None),
        P(("brick", "chan"), None),
        P(),
        P(("brick", "chan"), None, None),
    )
    return jax.shard_map(
        shards,
        mesh=mesh,
        in_specs=placed,
        out_specs=(P(("brick", "chan"), None, None), P(("brick", "chan"), None, None), P()),
        check_vma=False,
    )
```

profile of v0, /device:TPU:1, one launch (start us, length us, event | category | flops | bytes accessed | tf_op | source)
XLA Modules:
  0.0 660.9 jit_solution(16796859060458923091)
XLA Ops:
  7.2 1.1 copy.8
  9.8 8.8 %collective-permute-start.1 = (bf16[1,96,512]{1,2,0:T(8,128)(2,1)}, bf16[1,96,512]{1,2,0:T(8,128)(2,1)}, u32[]{:S(2)}, u32[]{:S(2)}) collective-permute-start(bf16[1,96,512]{1,2,0:T(8,128)(2,1)} %broadcast_multiply_fusion.1), channel_id=1, source_target_pairs={{1,0},{2,1},{3,2},{4,3},{5,4},{6,5},{7,6},{8,7},{9,8},{10,9},{11,1... | collective-permute-start | bytes 294920 | tf_op jit(solution)/shard_map/ppermute | solution.py:19
  18.6 1.9 collective-permute-start
  56.3 1.0 copy.9
  57.3 1.0 convolution_bitcast_fusion.26
  61.5 1.0 convolution_bitcast_fusion.21
  73.1 1.0 convolution_bitcast_fusion.9
  75.0 1.0 convolution_bitcast_fusion.7
  77.9 1.0 convolution_bitcast_fusion.4
  90.7 1.1 copy.12
  91.7 1.1 copy.13
  92.8 1.1 copy.14
  96.3 1.9 dynamic-slice_add_fusion
  98.2 2.2 scatter-add.189
  102.8 1.0 copy.21
  144.8 1.9 collective-permute-start.3
  147.5 3.0 collective-permute-start.2
  151.0 1.2 maximum_maximum_fusion
  178.7 1.0 copy-done.1
  179.8 1.1 convolution_bitcast_fusion.36
  181.0 1.6 multiply_convert_fusion
  182.6 2.2 fusion.14
  184.8 466.8 %all-reduce.4.cloned.1.call-done = f32[27,96,96]{2,1,0:T(8,128)} async-done(((f32[27,96,96]{2,1,0:T(8,128)}), f32[27,96,96]{2,1,0:T(8,128)}) %all-reduce.4.cloned.1.call-update) | async-done | bytes 995344 | tf_op jit(solution)/shard_map/psum | solution.py:106
  651.5 2.5 copy.146
  (355 shorter events, 86.4 us)
Async XLA Ops:
  7.2 51.2 %copy-start = (bf16[27,96,96]{2,1,0:T(8,128)(2,1)S(1)}, bf16[27,96,96]{2,1,0:T(8,128)(2,1)}, u32[]{:S(2)}) copy-start(bf16[27,96,96]{2,1,0:T(8,128)(2,1)} %param.184) | copy-start | bytes 1492996
  7.2 644.4 %all-reduce.4.cloned.1.call-start = ((), (), s32[]{:S(2)}) async-start(), calls=%async_computation | async-start | bytes 2654208 | tf_op jit(solution)/shard_map/psum | solution.py:106
  9.8 141.2 %collective-permute-start.1 = (bf16[1,96,512]{1,2,0:T(8,128)(2,1)}, bf16[1,96,512]{1,2,0:T(8,128)(2,1)}, u32[]{:S(2)}, u32[]{:S(2)}) collective-permute-start(bf16[1,96,512]{1,2,0:T(8,128)(2,1)} %broadcast_multiply_fusion.1), channel_id=1, source_target_pairs={{1,0},{2,1},{3,2},{4,3},{5,4},{6,5},{7,6},{8,7},{9,8},{10,9},{11,1... | collective-permute-start | bytes 294920 | tf_op jit(solution)/shard_map/ppermute | solution.py:19
  18.6 132.5 %collective-permute-start = (bf16[1,96,512]{1,2,0:T(8,128)(2,1)}, bf16[1,96,512]{1,2,0:T(8,128)(2,1)}, u32[]{:S(2)}, u32[]{:S(2)}) collective-permute-start(bf16[1,96,512]{1,2,0:T(8,128)(2,1)} %broadcast_multiply_fusion.1), channel_id=1, source_target_pairs={{0,1},{1,2},{2,3},{3,4},{4,5},{5,6},{6,7},{7,8},{8,9},{9,10},{10,1... | collective-permute-start | bytes 294920 | tf_op jit(solution)/shard_map/ppermute | solution.py:17
  94.7 5.7 copy-start.17
  94.7 5.8 copy-start.16
  100.8 1.3 copy-start.13
  102.4 1.8 copy-start.12
  102.4 1.9 copy-start.11
  104.6 1.3 copy-start.8
  106.2 1.3 copy-start.5
  107.8 1.3 copy-start.2
  111.2 7.7 %copy-start.28 = (s32[5]{0:T(128)S(1)}, s32[5]{0:T(128)}, u32[]{:S(2)}) copy-start(s32[5]{0:T(128)} %constant.2468.clone.1) | copy-start | bytes 64
  111.2 7.7 %copy-start.29 = (s32[5]{0:T(128)S(1)}, s32[5]{0:T(128)}, u32[]{:S(2)}) copy-start(s32[5]{0:T(128)} %constant.2469.clone.1) | copy-start | bytes 64
  111.2 16.6 %copy-start.26 = (s32[5]{0:T(128)S(1)}, s32[5]{0:T(128)}, u32[]{:S(2)}) copy-start(s32[5]{0:T(128)} %constant.2470.clone.1) | copy-start | bytes 64
  111.2 16.6 %copy-start.27 = (s32[5]{0:T(128)S(1)}, s32[5]{0:T(128)}, u32[]{:S(2)}) copy-start(s32[5]{0:T(128)} %constant.2471.clone.1) | copy-start | bytes 64
  111.2 21.6 %copy-start.30 = (s32[5]{0:T(128)S(1)}, s32[5]{0:T(128)}, u32[]{:S(2)}) copy-start(s32[5]{0:T(128)} %constant.2472.clone.1) | copy-start | bytes 64
  111.3 21.5 %copy-start.31 = (s32[5]{0:T(128)S(1)}, s32[5]{0:T(128)}, u32[]{:S(2)}) copy-start(s32[5]{0:T(128)} %constant.2473.clone.1) | copy-start | bytes 64
  143.9 6.8 %copy-start.22 = (s32[1,512]{1,0:T(1,128)S(1)}, s32[1,512]{1,0:T(1,128)}, u32[]{:S(2)}) copy-start(s32[1,512]{1,0:T(1,128)} %param.182) | copy-start | bytes 6148
  144.8 36.1 %collective-permute-start.3 = (bf16[1,96,512]{2,1,0:T(8,128)(2,1)}, bf16[1,96,512]{2,1,0:T(8,128)(2,1)}, u32[]{:S(2)}, u32[]{:S(2)}) collective-permute-start(bf16[1,96,512]{2,1,0:T(8,128)(2,1)} %copy.39), channel_id=1, source_target_pairs={{0,1},{1,2},{2,3},{3,4},{4,5},{5,6},{6,7},{7,8},{8,9},{9,10},{10,1... | collective-permute-start | bytes 294920 | tf_op jit(solution)/shard_map/ppermute | solution.py:29
  147.5 33.5 %collective-permute-start.2 = (bf16[1,96,512]{2,1,0:T(8,128)(2,1)}, bf16[1,96,512]{2,1,0:T(8,128)(2,1)}, u32[]{:S(2)}, u32[]{:S(2)}) collective-permute-start(bf16[1,96,512]{2,1,0:T(8,128)(2,1)} %copy.37), channel_id=1, source_target_pairs={{1,0},{2,1},{3,2},{4,3},{5,4},{6,5},{7,6},{8,7},{9,8},{10,9},{11,1... | collective-permute-start | bytes 294920 | tf_op jit(solution)/shard_map/ppermute | solution.py:29
  156.0 19.3 %copy-start.19 = (bf16[1,96,8,8,8]{1,4,3,2,0:T(8,128)(2,1)}, bf16[1,96,8,8,8]{1,4,3,2,0:T(8,128)(2,1)S(1)}, u32[]{:S(2)}) copy-start(bf16[1,96,8,8,8]{1,4,3,2,0:T(8,128)(2,1)S(1)} %get-tuple-element.1124) | copy-start | bytes 294916
  156.0 19.6 %copy-start.21 = (bf16[1,96,8,8,8]{1,4,3,2,0:T(8,128)(2,1)}, bf16[1,96,8,8,8]{1,4,3,2,0:T(8,128)(2,1)S(1)}, u32[]{:S(2)}) copy-start(bf16[1,96,8,8,8]{1,4,3,2,0:T(8,128)(2,1)S(1)} %get-tuple-element.1134) | copy-start | bytes 294916
  178.7 3.8 copy-start.20
  (15 other events, 15.5 us)
Sparse Core Ops, SparseCore 0:
  179.9 471.5 all-reduce.3
where the time goes:
time: 663 us; the launch traced here: 661 us
  waiting for transfers between devices  467 us (70%)
  between operations  67.1 us (10%)
  matrix products  48.2 us (7%)
  local copies, waits for them, and re-layouts  34.7 us (5%)
  other arithmetic  28.4 us (4%)
  starting transfers between devices  15.7 us (2%)
    psum x1, waiting for transfers between devices, shards(): grad_weight = lax.psum(jnp.stack(tap_grads, axis=0), ('brick', 'chan'))  467 us
    dot_general x27, matrix products, backward_cells(): jnp.einsum('co,bov->bcv', weight[tap], cotan, preferred_element_type=jnp....  22.7 us
    dot_general x27, matrix products, shards(): jnp.einsum('co,bcv->bov', weight[tap], window, preferred_element_type=jnp...  17.3 us
    another operation x23, other arithmetic  14.5 us
  transfers between devices with their start and end apart: 5, of which 1 were waited for; matrix products, arithmetic and copies ran while one was open for 16% of the time, Pallas kernels for 0%

commit v1 on v0

v1 whole, which is shorter than its diff:
```python
import jax
import jax.numpy as jnp
from jax import lax
from jax.experimental import pallas as pl
from jax.experimental.pallas import tpu as pltpu
from jax.sharding import PartitionSpec as P

AXES = ("brick", "chan")
SIGNS = (-1, 0, 1)
VOXELS, LANES, CODES = 512, 128, 32
VMEM = pl.BlockSpec(memory_space=pltpu.VMEM)
SMEM = pl.BlockSpec(memory_space=pltpu.SMEM)
LIMIT = 32 * 1024 * 1024


def voxel_rows(block, occupied):
    masked = block.astype(jnp.float32) * occupied
    spare = jnp.zeros((LANES - masked.shape[0], masked.shape[1]), jnp.float32)
    return jnp.concatenate([masked, spare], axis=0).T


def pack_kernel(neighbors, occupancy, features, grad_output, cotangent, masked):
    occupied = occupancy[...].astype(jnp.float32)
    cotangent[:VOXELS, :] = voxel_rows(grad_output[0], occupied).astype(jnp.bfloat16)
    masked[...] = voxel_rows(features[0], occupied).astype(jnp.bfloat16)
    own = neighbors[0, 13]
    row = lax.broadcasted_iota(jnp.int32, (CODES, LANES), 0)
    codes = jnp.full((CODES, LANES), 2, jnp.int32)
    for offset in range(27):
        brick = neighbors[0, offset]
        codes = jnp.where(row == offset, jnp.where(brick < 0, 2, brick - own), codes)
    cotangent[VOXELS:, :] = codes.astype(jnp.float32).astype(jnp.bfloat16)


def faces(sign):
    if sign < 0:
        return slice(7, 8), slice(0, 1)
    if sign > 0:
        return slice(0, 1), slice(9, 10)
    return slice(0, 8), slice(1, 9)


def offset_id(x, y, z):
    return 9 * (x + 1) + 3 * (y + 1) + (z + 1)


def build_windows(bricks, own, weigh, columns, windows):
    for x in SIGNS:
        from_x, to_x = faces(x)
        for y in SIGNS:
            from_y, to_y = faces(y)
            parts = [brick[from_x, from_y] for brick in bricks]
            shape = parts[0].shape

            def side(z):
                return sum(part * scale for part, scale in zip(parts, weigh(x, y, z)))

            middle = parts[own] if x == 0 and y == 0 else side(0)
            middle = middle.reshape(-1, 8, LANES)
            below = side(-1).reshape(-1, 8, LANES)
            above = side(1).reshape(-1, 8, LANES)
            row = lax.broadcasted_iota(jnp.int32, middle.shape, 1)
            columns[0, to_x, to_y] = pltpu.roll(jnp.where(row == 7, below, middle), 1, 1).reshape(shape)
            columns[1, to_x, to_y] = middle.reshape(shape)
            columns[2, to_x, to_y] = pltpu.roll(jnp.where(row == 0, above, middle), 7, 1).reshape(shape)
    for dy in range(3):
        for dz in range(3):
            tap = 3 * dy + dz
            for px in range(10):
                windows[px, :, tap * LANES:(tap + 1) * LANES] = (
                    columns[dz, px, dy:dy + 8].reshape(64, LANES).astype(jnp.bfloat16)
                )


def rows_of(ref):
    return ref[:VOXELS, :].astype(jnp.float32).reshape(8, 8, 8, LANES)


def returned_scales(own, before, after):
    tables = [ref[VOXELS:, :].astype(jnp.float32) for ref in (before, own, after)]

    def weigh(x, y, z):
        at = offset_id(-x, -y, -z)
        return [
            jnp.where(table[at:at + 1] == code, 1.0, 0.0)
            for table, code in zip(tables, (1.0, 0.0, -1.0))
        ]

    return weigh


def read_scales(own):
    table = own[VOXELS:, :].astype(jnp.float32)

    def weigh(x, y, z):
        at = offset_id(x, y, z)
        return [jnp.where(table[at:at + 1] == code, 1.0, 0.0) for code in (-1.0, 0.0, 1.0)]

    return weigh


def span(windows, dx):
    return windows[dx:dx + 8].reshape(VOXELS, 9 * LANES)


def weight_grad_kernel(features, occupancy, own, before, after, grad, columns, windows):
    depth = features.shape[1]
    bricks = [rows_of(ref) for ref in (before, own, after)]
    build_windows(bricks, 1, returned_scales(own, before, after), columns, windows)
    masked = (features[0].astype(jnp.float32) * occupancy[...].astype(jnp.float32)).astype(jnp.bfloat16)
    for dx in range(3):
        product = jnp.dot(masked, span(windows, dx), preferred_element_type=jnp.float32)
        for tap in range(9):
            grad[26 - (9 * dx + tap)] = product[:, tap * LANES:tap * LANES + depth].astype(grad.dtype)


def outputs_kernel(
    occupancy, weight, own, before, after, masked, masked_before, masked_after,
    output, grad_features, columns, windows, taps,
):
    depth = weight.shape[1]
    occupied = occupancy[...].astype(jnp.float32)
    taps[...] = jnp.zeros_like(taps)
    for tap in range(27):
        taps[tap, :depth, :depth] = weight[tap]

    def finish(rows):
        return (rows.T[:depth] * occupied).astype(jnp.bfloat16)

    bricks = [rows_of(ref) for ref in (masked_before, masked, masked_after)]
    build_windows(bricks, 1, read_scales(own), columns, windows)
    total = jnp.zeros((VOXELS, LANES), jnp.float32)
    for dx in range(3):
        kernel = taps[9 * dx:9 * dx + 9].reshape(9 * LANES, LANES)
        total = total + jnp.dot(span(windows, dx), kernel, preferred_element_type=jnp.float32)
    output[0] = finish(total)

    bricks = [rows_of(ref) for ref in (before, own, after)]
    build_windows(bricks, 1, returned_scales(own, before, after), columns, windows)
    total = jnp.zeros((VOXELS, LANES), jnp.float32)
    for dx in range(3):
        for tap in range(9):
            total = total + lax.dot_general(
                windows[dx:dx + 8, :, tap * LANES:(tap + 1) * LANES].reshape(VOXELS, LANES),
                taps[26 - (9 * dx + tap)],
                (((1,), (1,)), ((), ())),
                preferred_element_type=jnp.float32,
            )
    grad_features[0] = finish(total)


WINDOW_SCRATCH = [
    pltpu.VMEM((3, 10, 10, 8, LANES), jnp.float32),
    pltpu.VMEM((10, 64, 9 * LANES), jnp.bfloat16),
]


def both_ways(block):
    count = lax.axis_size("brick") * lax.axis_size("chan")
    before = lax.ppermute(block, AXES, [(i, i + 1) for i in range(count - 1)])
    after = lax.ppermute(block, AXES, [(i + 1, i) for i in range(count - 1)])
    return before, after


def total_over_devices(grad):
    return lax.psum(grad, AXES)


def shards(features, occupancy, neighbors, weight, grad_output):
    depth = features.shape[1]
    cotangent, masked = pl.pallas_call(
        pack_kernel,
        out_shape=[
            jax.ShapeDtypeStruct((VOXELS + CODES, LANES), jnp.bfloat16),
            jax.ShapeDtypeStruct((VOXELS, LANES), jnp.bfloat16),
        ],
        in_specs=[SMEM, VMEM, VMEM, VMEM],
        out_specs=[VMEM, VMEM],
        name="pack",
    )(neighbors, occupancy, features, grad_output)
    before, after = both_ways(cotangent)
    masked_before, masked_after = both_ways(masked)
    grad = pl.pallas_call(
        weight_grad_kernel,
        out_shape=jax.ShapeDtypeStruct((27, depth, depth), jnp.float32),
        in_specs=[VMEM] * 5,
        out_specs=VMEM,
        scratch_shapes=WINDOW_SCRATCH,
        compiler_params=pltpu.CompilerParams(vmem_limit_bytes=LIMIT),
        cost_estimate=pl.CostEstimate(flops=27 * 2 * 128 * 128 * 512, bytes_accessed=2 * 1024 * 1024, transcendentals=0),
        name="weight_grad",
    )(features, occupancy, cotangent, before, after)
    grad_weight = total_over_devices(grad)
    output, grad_features = pl.pallas_call(
        outputs_kernel,
        out_shape=[jax.ShapeDtypeStruct(features.shape, jnp.bfloat16)] * 2,
        in_specs=[VMEM] * 8,
        out_specs=[VMEM, VMEM],
        scratch_shapes=WINDOW_SCRATCH + [pltpu.VMEM((27, LANES, LANES), jnp.bfloat16)],
        compiler_params=pltpu.CompilerParams(vmem_limit_bytes=LIMIT),
        cost_estimate=pl.CostEstimate(flops=54 * 2 * 128 * 128 * 512, bytes_accessed=2 * 1024 * 1024, transcendentals=0),
        name="outputs",
    )(occupancy, weight, cotangent, before, after, masked, masked_before, masked_after)
    return output, grad_features, grad_weight


def solution(mesh):
    split = P(AXES, None, None)
    flat = P(AXES, None)
    return jax.shard_map(
        shards,
        mesh=mesh,
        in_specs=(split, flat, flat, P(), split),
        out_specs=(split, split, P()),
        check_vma=False,
    )
```

time: 663 us -> 509 us (0.77)
  between operations: 67.1 us -> 14.1 us
  matrix products: 48.2 us -> 0 us
  local copies, waits for them, and re-layouts: 34.7 us -> 4.96 us
  other arithmetic: 28.4 us -> 0 us
  Pallas kernels: 0 us -> 7.28 us
    dot_general x81 -> x0, matrix products: 48.2 us -> none  [the longest x27 22.7 us: backward_cells(): jnp.einsum('co,bov->bcv', weight[tap], cotan, preferred_element_type=jnp....]
    another operation x23 -> x0, other arithmetic: 14.5 us -> none
    scatter-add x37 -> x0, local copies, waits for them, and re-layouts: 9.13 us -> none  [the longest x19 7.97 us: backward_cells(): grad_padded = grad_padded.at[:, :, low_x:low_x + 8, low_y:low_y + 8, low_...]
    pallas_call x0 -> x3, Pallas kernels: none -> 7.28 us  [the longest x1 3.48 us: shards(): pl.pallas_call(outputs_kernel, out_shape=[jax.ShapeDtypeStruct(features.s...]
    transpose x27 -> x0, local copies, waits for them, and re-layouts: 7 us -> none  [backward_cells(): jnp.einsum('co,bov->bcv', weight[tap], cotan, preferred_element_type=jnp....]
  transfers between devices with their start and end apart: 5 -> 5, of which waited for: 1 -> 4; matrix products, arithmetic and copies ran while one was open for 16% -> 0% of each run, Pallas kernels for 0% -> 1%
where the time goes in v1:
time: 509 us
  waiting for transfers between devices  466 us (92%)
  starting transfers between devices  16.9 us (3%)
  between operations  14.1 us (3%)
  Pallas kernels  7.28 us (1%)
    psum x1, waiting for transfers between devices, total_over_devices(): return lax.psum(grad, AXES)  462 us
    ppermute x2, starting transfers between devices, both_ways(): after = lax.ppermute(block, AXES, [(i + 1, i) for i in range(count - 1)])  10.7 us
  transfers between devices with their start and end apart: 5, of which 4 were waited for; matrix products, arithmetic and copies ran while one was open for 0% of the time, Pallas kernels for 1%

profile of v1, /device:TPU:1, one launch (start us, length us, event | category | flops | bytes accessed | tf_op | source)
XLA Modules:
  0.0 509.1 jit_solution(2292344177882778945)
XLA Ops:
  7.2 0.0 all-reduce.2.cloned.1.call-start
  7.2 0.0 copy-start.4
  7.2 1.8 pack.1
  9.0 8.8 %collective-permute-start.1 = (bf16[544,128]{1,0:T(8,128)(2,1)}, bf16[544,128]{1,0:T(8,128)(2,1)S(1)}, u32[]{:S(2)}, u32[]{:S(2)}) collective-permute-start(bf16[544,128]{1,0:T(8,128)(2,1)} %get-tuple-element.7.own), channel_id=1, source_target_pairs={{1,0},{2,1},{3,2},{4,3},{5,4},{6,5},{7,6},{8,7},{9,8},{10,9},{11,1... | collective-permute-start | bytes 417800 | tf_op jit(solution)/shard_map/ppermute | solution.py:161
  17.8 1.9 collective-permute-start
  19.7 0.0 collective-permute-done.1.after
  19.7 2.3 collective-permute-done.before
  22.0 0.0 copy-start
  22.0 0.9 copy-done
  22.9 0.9 copy-done.1
  23.8 0.7 copy-done.3
  24.5 2.0 weight_grad.1
  26.5 0.0 all-reduce.2.cloned.1.call-update
  26.6 0.0 copy-done.6
  26.6 1.9 collective-permute-start.3
  28.5 4.3 collective-permute-start.2
  32.8 0.7 collective-permute-done.3.masked_after
  33.5 1.2 collective-permute-done.2.masked_before
  34.7 0.0 copy-done.4
  34.7 0.0 copy-done.2
  34.7 0.0 copy-done.5
  34.7 3.5 outputs.1
  38.2 461.6 %all-reduce.2.cloned.1.call-done = f32[27,96,96]{2,1,0:T(8,128)} async-done(((f32[27,96,96]{2,1,0:T(8,128)}), f32[27,96,96]{2,1,0:T(8,128)}) %all-reduce.2.cloned.1.call-update) | async-done | bytes 995344 | tf_op jit(solution)/shard_map/psum | solution.py:166
  499.8 2.5 copy.9
  (5 shorter events, 0.0 us)
Async XLA Ops:
  7.2 492.6 %all-reduce.2.cloned.1.call-start = ((), (), s32[]{:S(2)}) async-start(), calls=%async_computation | async-start | bytes 2654208 | tf_op jit(solution)/shard_map/psum | solution.py:166
  7.2 27.5 %copy-start.4 = (s32[1,512]{1,0:T(1,128)S(1)}, s32[1,512]{1,0:T(1,128)}, u32[]{:S(2)}) copy-start(s32[1,512]{1,0:T(1,128)} %occupancy.5) | copy-start | bytes 6148
  9.0 10.7 %collective-permute-start.1 = (bf16[544,128]{1,0:T(8,128)(2,1)}, bf16[544,128]{1,0:T(8,128)(2,1)S(1)}, u32[]{:S(2)}, u32[]{:S(2)}) collective-permute-start(bf16[544,128]{1,0:T(8,128)(2,1)} %get-tuple-element.7.own), channel_id=1, source_target_pairs={{1,0},{2,1},{3,2},{4,3},{5,4},{6,5},{7,6},{8,7},{9,8},{10,9},{11,1... | collective-permute-start | bytes 417800 | tf_op jit(solution)/shard_map/ppermute | solution.py:161
  17.8 4.2 collective-permute-start
  22.0 0.9 copy-start
  22.9 0.9 copy-start.1
  23.8 0.7 copy-start.3
  24.5 2.1 copy-start.6
  24.5 10.2 %copy-start.2 = (bf16[544,128]{1,0:T(8,128)(2,1)S(1)}, bf16[544,128]{1,0:T(8,128)(2,1)}, u32[]{:S(2)}) copy-start(bf16[544,128]{1,0:T(8,128)(2,1)} %get-tuple-element.7.own) | copy-start | bytes 417796
  24.5 10.2 %copy-start.5 = (bf16[27,96,96]{2,1,0:T(8,128)(2,1)S(1)}, bf16[27,96,96]{2,1,0:T(8,128)(2,1)}, u32[]{:S(2)}) copy-start(bf16[27,96,96]{2,1,0:T(8,128)(2,1)} %weight.1) | copy-start | bytes 1492996
  26.6 6.9 %collective-permute-start.3 = (bf16[512,128]{1,0:T(8,128)(2,1)S(1)}, bf16[512,128]{1,0:T(8,128)(2,1)S(1)}, u32[]{:S(2)}, u32[]{:S(2)}) collective-permute-start(bf16[512,128]{1,0:T(8,128)(2,1)S(1)} %copy-done.6), channel_id=1, source_target_pairs={{1,0},{2,1},{3,2},{4,3},{5,4},{6,5},{7,6},{8,7},{9,8},{10,9},{11,1... | collective-permute-start | bytes 393224 | tf_op jit(solution)/shard_map/ppermute | solution.py:161
  28.5 6.2 %collective-permute-start.2 = (bf16[512,128]{1,0:T(8,128)(2,1)S(1)}, bf16[512,128]{1,0:T(8,128)(2,1)S(1)}, u32[]{:S(2)}, u32[]{:S(2)}) collective-permute-start(bf16[512,128]{1,0:T(8,128)(2,1)S(1)} %copy-done.6), channel_id=1, source_target_pairs={{0,1},{1,2},{2,3},{3,4},{4,5},{5,6},{6,7},{7,8},{8,9},{9,10},{10,1... | collective-permute-start | bytes 393224 | tf_op jit(solution)/shard_map/ppermute | solution.py:160
Sparse Core Ops, SparseCore 0:
  26.7 473.0 all-reduce.1

commit v2 on v1

--- a/solution.py
+++ b/solution.py
@@ -8,6 +8,8 @@
 AXES = ("brick", "chan")
 SIGNS = (-1, 0, 1)
 VOXELS, LANES, CODES = 512, 128, 32
+ROWS = 2048
+NEAR, FAR = 64, 8
 VMEM = pl.BlockSpec(memory_space=pltpu.VMEM)
 SMEM = pl.BlockSpec(memory_space=pltpu.SMEM)
 LIMIT = 32 * 1024 * 1024
@@ -19,17 +21,17 @@
     return jnp.concatenate([masked, spare], axis=0).T
 
 
-def pack_kernel(neighbors, occupancy, features, grad_output, cotangent, masked):
+def pack_kernel(neighbors, occupancy, features, grad_output, packed):
     occupied = occupancy[...].astype(jnp.float32)
-    cotangent[:VOXELS, :] = voxel_rows(grad_output[0], occupied).astype(jnp.bfloat16)
-    masked[...] = voxel_rows(features[0], occupied).astype(jnp.bfloat16)
+    packed[:VOXELS, :] = voxel_rows(grad_output[0], occupied).astype(jnp.bfloat16)
+    packed[VOXELS:2 * VOXELS, :] = voxel_rows(features[0], occupied).astype(jnp.bfloat16)
     own = neighbors[0, 13]
     row = lax.broadcasted_iota(jnp.int32, (CODES, LANES), 0)
     codes = jnp.full((CODES, LANES), 2, jnp.int32)
     for offset in range(27):
         brick = neighbors[0, offset]
         codes = jnp.where(row == offset, jnp.where(brick < 0, 2, brick - own), codes)
-    cotangent[VOXELS:, :] = codes.astype(jnp.float32).astype(jnp.bfloat16)
+    packed[2 * VOXELS:, :] = codes.astype(jnp.float32).astype(jnp.bfloat16)
 
 
 def faces(sign):
@@ -72,12 +74,20 @@
                 )
 
 
-def rows_of(ref):
+def cotangent_of(ref):
     return ref[:VOXELS, :].astype(jnp.float32).reshape(8, 8, 8, LANES)
 
 
+def masked_of(ref):
+    return ref[VOXELS:2 * VOXELS, :].astype(jnp.float32).reshape(8, 8, 8, LANES)
+
+
+def codes_of(ref):
+    return ref[2 * VOXELS:, :].astype(jnp.float32)
+
+
 def returned_scales(own, before, after):
-    tables = [ref[VOXELS:, :].astype(jnp.float32) for ref in (before, own, after)]
+    tables = [codes_of(ref) for ref in (before, own, after)]
 
     def weigh(x, y, z):
         at = offset_id(-x, -y, -z)
@@ -90,7 +100,7 @@
 
 
 def read_scales(own):
-    table = own[VOXELS:, :].astype(jnp.float32)
+    table = codes_of(own)
 
     def weigh(x, y, z):
         at = offset_id(x, y, z)
@@ -103,20 +113,48 @@
     return windows[dx:dx + 8].reshape(VOXELS, 9 * LANES)
 
 
-def weight_grad_kernel(features, occupancy, own, before, after, grad, columns, windows):
-    depth = features.shape[1]
-    bricks = [rows_of(ref) for ref in (before, own, after)]
+def dense_rows(block):
+    lane = lax.broadcasted_iota(jnp.int32, (72, LANES), 1)
+    tail = jnp.concatenate([pltpu.roll(block[72:], 96 - 32 * third, 1) for third in range(3)], axis=0)
+    return jnp.where(lane < 96, block[:72], tail)
+
+
+def square_rows(dense):
+    lane = lax.broadcasted_iota(jnp.int32, (24, LANES), 1)
+    thirds = [pltpu.roll(dense[24 * third:24 * third + 24], 32 + 32 * third, 1) for third in range(3)]
+    tail = jnp.where(lane < 32, thirds[0], jnp.where(lane < 64, thirds[1], thirds[2]))
+    return jnp.concatenate([dense, tail], axis=0)[:, :96]
+
+
+def weight_grad_kernel(features, occupancy, own, before, after, grad, columns, windows, dense):
+    bricks = [cotangent_of(ref) for ref in (before, own, after)]
     build_windows(bricks, 1, returned_scales(own, before, after), columns, windows)
     masked = (features[0].astype(jnp.float32) * occupancy[...].astype(jnp.float32)).astype(jnp.bfloat16)
     for dx in range(3):
         product = jnp.dot(masked, span(windows, dx), preferred_element_type=jnp.float32)
         for tap in range(9):
-            grad[26 - (9 * dx + tap)] = product[:, tap * LANES:tap * LANES + depth].astype(grad.dtype)
+            at = 72 * (26 - (9 * dx + tap))
+            dense[at:at + 72] = dense_rows(product[:, tap * LANES:(tap + 1) * LANES])
+    dense[27 * 72:] = jnp.zeros((ROWS - 27 * 72, LANES), jnp.float32)
+    grad[...] = dense[...].astype(jnp.bfloat16).reshape(grad.shape)
+
+
+def sum_kernel(parts, copies):
+    total = parts[0].astype(jnp.float32)
+    for part in range(1, parts.shape[0]):
+        total = total + parts[part].astype(jnp.float32)
+    for copy in range(copies.shape[0]):
+        copies[copy] = total.astype(copies.dtype)
+
+
+def unpack_kernel(dense, grad):
+    rows = dense[...].reshape(ROWS, LANES).astype(jnp.float32)
+    for tap in range(27):
+        grad[tap] = square_rows(rows[72 * tap:72 * tap + 72])
 
 
 def outputs_kernel(
-    occupancy, weight, own, before, after, masked, masked_before, masked_after,
-    output, grad_features, columns, windows, taps,
+    occupancy, weight, own, before, after, output, grad_features, columns, windows, taps,
 ):
     depth = weight.shape[1]
     occupied = occupancy[...].astype(jnp.float32)
@@ -127,7 +165,7 @@
     def finish(rows):
         return (rows.T[:depth] * occupied).astype(jnp.bfloat16)
 
-    bricks = [rows_of(ref) for ref in (masked_before, masked, masked_after)]
+    bricks = [masked_of(ref) for ref in (before, own, after)]
     build_windows(bricks, 1, read_scales(own), columns, windows)
     total = jnp.zeros((VOXELS, LANES), jnp.float32)
     for dx in range(3):
@@ -135,7 +173,7 @@
         total = total + jnp.dot(span(windows, dx), kernel, preferred_element_type=jnp.float32)
     output[0] = finish(total)
 
-    bricks = [rows_of(ref) for ref in (before, own, after)]
+    bricks = [cotangent_of(ref) for ref in (before, own, after)]
     build_windows(bricks, 1, returned_scales(own, before, after), columns, windows)
     total = jnp.zeros((VOXELS, LANES), jnp.float32)
     for dx in range(3):
@@ -162,45 +200,55 @@
     return before, after
 
 
+def call(kernel, name, shapes, operands, specs=None, scratch=(), flops=0):
+    return pl.pallas_call(
+        kernel,
+        out_shape=shapes,
+        in_specs=specs or [VMEM] * len(operands),
+        out_specs=jax.tree.map(lambda _: VMEM, shapes),
+        scratch_shapes=list(scratch),
+        compiler_params=pltpu.CompilerParams(vmem_limit_bytes=LIMIT),
+        cost_estimate=pl.CostEstimate(flops=flops, bytes_accessed=2 * 1024 * 1024, transcendentals=0),
+        name=name,
+    )(*operands)
+
+
+def bf16(*shape):
+    return jax.ShapeDtypeStruct(shape, jnp.bfloat16)
+
+
 def total_over_devices(grad):
-    return lax.psum(grad, AXES)
+    rows = grad.shape[1]
+    count = NEAR * FAR
+    near = [[first + i for i in range(NEAR)] for first in range(0, count, NEAR)]
+    far = [[first + NEAR * i for i in range(FAR)] for first in range(NEAR)]
+    pieces = lax.all_to_all(grad, AXES, 0, 0, tiled=True, axis_index_groups=near)
+    share = call(sum_kernel, "sum_near", bf16(FAR, rows, LANES), (pieces,))
+    shares = lax.all_to_all(share, AXES, 0, 0, tiled=True, axis_index_groups=far)
+    whole = call(sum_kernel, "sum_far", bf16(NEAR, rows, LANES), (shares,))
+    return lax.all_to_all(whole, AXES, 0, 0, tiled=True, axis_index_groups=near)
 
 
 def shards(features, occupancy, neighbors, weight, grad_output):
     depth = features.shape[1]
-    cotangent, masked = pl.pallas_call(
-        pack_kernel,
-        out_shape=[
-            jax.ShapeDtypeStruct((VOXELS + CODES, LANES), jnp.bfloat16),
-            jax.ShapeDtypeStruct((VOXELS, LANES), jnp.bfloat16),
-        ],
-        in_specs=[SMEM, VMEM, VMEM, VMEM],
-        out_specs=[VMEM, VMEM],
-        name="pack",
-    )(neighbors, occupancy, features, grad_output)
-    before, after = both_ways(cotangent)
-    masked_before, masked_after = both_ways(masked)
-    grad = pl.pallas_call(
-        weight_grad_kernel,
-        out_shape=jax.ShapeDtypeStruct((27, depth, depth), jnp.float32),
-        in_specs=[VMEM] * 5,
-        out_specs=VMEM,
-        scratch_shapes=WINDOW_SCRATCH,
-        compiler_params=pltpu.CompilerParams(vmem_limit_bytes=LIMIT),
-        cost_estimate=pl.CostEstimate(flops=27 * 2 * 128 * 128 * 512, bytes_accessed=2 * 1024 * 1024, transcendentals=0),
-        name="weight_grad",
-    )(features, occupancy, cotangent, before, after)
-    grad_weight = total_over_devices(grad)
-    output, grad_features = pl.pallas_call(
-        outputs_kernel,
-        out_shape=[jax.ShapeDtypeStruct(features.shape, jnp.bfloat16)] * 2,
-        in_specs=[VMEM] * 8,
-        out_specs=[VMEM, VMEM],
-        scratch_shapes=WINDOW_SCRATCH + [pltpu.VMEM((27, LANES, LANES), jnp.bfloat16)],
-        compiler_params=pltpu.CompilerParams(vmem_limit_bytes=LIMIT),
-        cost_estimate=pl.CostEstimate(flops=54 * 2 * 128 * 128 * 512, bytes_accessed=2 * 1024 * 1024, transcendentals=0),
-        name="outputs",
-    )(occupancy, weight, cotangent, before, after, masked, masked_before, masked_after)
+    own = call(
+        pack_kernel, "pack", bf16(2 * VOXELS + CODES, LANES),
+        (neighbors, occupancy, features, grad_output), [SMEM, VMEM, VMEM, VMEM],
+    )
+    before, after = both_ways(own)
+    dot = 27 * 2 * LANES * LANES * VOXELS
+    grad = call(
+        weight_grad_kernel, "weight_grad", bf16(NEAR, ROWS // NEAR, LANES),
+        (features, occupancy, own, before, after),
+        scratch=WINDOW_SCRATCH + [pltpu.VMEM((ROWS, LANES), jnp.float32)], flops=dot,
+    )
+    grad = total_over_devices(grad)
+    output, grad_features = call(
+        outputs_kernel, "outputs", [bf16(*features.shape)] * 2,
+        (occupancy, weight, own, before, after),
+        scratch=WINDOW_SCRATCH + [pltpu.VMEM((27, LANES, LANES), jnp.bfloat16)], flops=2 * dot,
+    )
+    grad_weight = call(unpack_kernel, "unpack", jax.ShapeDtypeStruct((27, depth, depth), jnp.float32), (grad,))
     return output, grad_features, grad_weight
 
 

time: 509 us -> 90 us (0.18)
  waiting for transfers between devices: 466 us -> 12.2 us
  blocking collectives: 0 us -> 49 us
  between operations: 14.1 us -> 0.7 us
    psum x1 -> x0, waiting for transfers between devices: 462 us -> none  [total_over_devices(): return lax.psum(grad, AXES)]
    all_to_all x0 -> x2, blocking collectives: none -> 49 us  [the longest x1 27.8 us: total_over_devices(): lax.all_to_all(share, AXES, 0, 0, tiled=True, axis_index_groups=far)]
    all_to_all x0 -> x1, waiting for transfers between devices: none -> 8.79 us  [total_over_devices(): return lax.all_to_all(whole, AXES, 0, 0, tiled=True, axis_index_groups=near)]
    all_to_all x0 -> x1, starting transfers between devices: none -> 6.5 us  [total_over_devices(): return lax.all_to_all(whole, AXES, 0, 0, tiled=True, axis_index_groups=near)]
    ppermute x2 -> x1, starting transfers between devices: 10.7 us -> 8.79 us  [both_ways(): after = lax.ppermute(block, AXES, [(i + 1, i) for i in range(count - 1)])]
  transfers between devices with their start and end apart: 5 -> 3, of which waited for: 4 -> 2; matrix products, arithmetic and copies ran while one was open for 0% -> 0% of each run, Pallas kernels for 1% -> 4%
where the time goes in v2:
time: 90 us; the launch traced here: 89.6 us
  blocking collectives  49 us (54%)
  starting transfers between devices  17.2 us (19%)
  waiting for transfers between devices  12.2 us (14%)
  Pallas kernels  7.37 us (8%)
  local copies, waits for them, and re-layouts  3.12 us (3%)
    all_to_all x1, blocking collectives, total_over_devices(): lax.all_to_all(share, AXES, 0, 0, tiled=True, axis_index_groups=far)  27.8 us
    all_to_all x1, blocking collectives, total_over_devices(): lax.all_to_all(grad, AXES, 0, 0, tiled=True, axis_index_groups=near)  21.2 us
    ppermute x1, starting transfers between devices, both_ways(): after = lax.ppermute(block, AXES, [(i + 1, i) for i in range(count - 1)])  8.79 us
    all_to_all x1, waiting for transfers between devices, total_over_devices(): return lax.all_to_all(whole, AXES, 0, 0, tiled=True, axis_index_groups=near)  8.79 us
    pallas_call x6, Pallas kernels, call(): pl.pallas_call(kernel, out_shape=shapes, in_specs=specs or [VMEM] * len(o...  7.37 us
    all_to_all x1, starting transfers between devices, total_over_devices(): return lax.all_to_all(whole, AXES, 0, 0, tiled=True, axis_index_groups=near)  6.5 us
    ppermute x1, waiting for transfers between devices, both_ways(): before = lax.ppermute(block, AXES, [(i, i + 1) for i in range(count - 1)])  3.37 us
    unnamed x12, local copies, waits for them, and re-layouts  3.12 us
  transfers between devices with their start and end apart: 3, of which 2 were waited for; matrix products, arithmetic and copies ran while one was open for 0% of the time, Pallas kernels for 4%

profile of v2, /device:TPU:1, one launch (start us, length us, event | category | flops | bytes accessed | tf_op | source)
XLA Modules:
  0.0 89.6 jit_solution(2936724782570736792)
XLA Ops:
  0.6 0.0 copy-start
  0.6 0.9 copy-done
  1.5 0.0 copy-start.1
  1.5 0.9 copy-done.1
  2.4 0.0 copy-start.2
  2.4 0.7 copy-done.2
  3.1 0.0 copy-start.4
  3.1 0.7 copy-done.4
  3.8 0.7 pack.1.own
  4.4 8.8 %collective-permute-start.1 = (bf16[1056,128]{1,0:T(8,128)(2,1)S(1)}, bf16[1056,128]{1,0:T(8,128)(2,1)S(1)}, u32[]{:S(2)}, u32[]{:S(2)}) collective-permute-start(bf16[1056,128]{1,0:T(8,128)(2,1)S(1)} %pack.1.own), channel_id=1, source_target_pairs={{1,0},{2,1},{3,2},{4,3},{5,4},{6,5},{7,6},{8,7},{9,8},{10,9},{11,1... | collective-permute-start | bytes 811016 | tf_op jit(solution)/shard_map/ppermute | solution.py:199
  13.2 1.9 %collective-permute-start = (bf16[1056,128]{1,0:T(8,128)(2,1)S(1)}, bf16[1056,128]{1,0:T(8,128)(2,1)S(1)}, u32[]{:S(2)}, u32[]{:S(2)}) collective-permute-start(bf16[1056,128]{1,0:T(8,128)(2,1)S(1)} %pack.1.own), channel_id=1, source_target_pairs={{0,1},{1,2},{2,3},{3,4},{4,5},{5,6},{6,7},{7,8},{8,9},{9,10},{10,1... | collective-permute-start | bytes 811016 | tf_op jit(solution)/shard_map/ppermute | solution.py:198
  15.2 0.0 collective-permute-done.1.after
  15.2 3.4 %collective-permute-done.before = bf16[1056,128]{1,0:T(8,128)(2,1)S(1)} collective-permute-done((bf16[1056,128]{1,0:T(8,128)(2,1)S(1)}, bf16[1056,128]{1,0:T(8,128)(2,1)S(1)}, u32[]{:S(2)}, u32[]{:S(2)}) %collective-permute-start) | collective-permute-done | bytes 270368 | tf_op jit(solution)/shard_map/ppermute | solution.py:198
  18.5 1.0 %weight_grad.1 = bf16[64,32,128]{2,1,0:T(8,128)(2,1)S(1)} custom-call(bf16[1,96,512]{2,1,0:T(8,128)(2,1)S(1)} %copy-done.1, s32[1,512]{1,0:T(1,128)S(1)} %copy-done.2, bf16[1056,128]{1,0:T(8,128)(2,1)S(1)} %pack.1.own, bf16[1056,128]{1,0:T(8,128)(2,1)S(1)} %collective-permute-done.before, bf16[1056,128]{1,0:T(8,128)(2,1)S(1)} %collective-permute-done.1.after), custom_call_target="tpu_custom_call" | custom-call | flops 452984832 | bytes 2097152 | tf_op jit(solution)/shard_map/weight_grad/pallas_call | solution.py:204
  19.6 21.2 %all_to_all.15.parts = bf16[64,32,128]{2,1,0:T(8,128)(2,1)S(1)} all-to-all(bf16[64,32,128]{2,1,0:T(8,128)(2,1)S(1)} %weight_grad.1), channel_id=1, replica_groups={{0,1,2,3,4,5,6,7,8,9,10,11,12,13,14,15,16,17,18,19,20,21,22,23,24,25,26..., dimensions={0} | all-to-all | bytes 1048576 | tf_op jit(solution)/shard_map/all_to_all | solution.py:225
  40.8 0.1 sum_near.1
  40.9 27.8 %all_to_all.16.parts = bf16[8,32,128]{2,1,0:T(8,128)(2,1)S(1)} all-to-all(bf16[8,32,128]{2,1,0:T(8,128)(2,1)S(1)} %sum_near.1), channel_id=1, replica_groups={{0,64,128,192,256,320,384,448},{1,65,129,193,257,321,385,449},{2,66,130..., dimensions={0} | all-to-all | bytes 131072 | tf_op jit(solution)/shard_map/all_to_all | solution.py:227
  68.7 0.8 sum_far.1
  69.5 6.5 %all-to-all-start.2 = ((bf16[64,32,128]{2,1,0:T(8,128)(2,1)}), bf16[64,32,128]{2,1,0:T(8,128)(2,1)S(1)}, u32[]{:S(2)}, u32[]{:S(2)}) async-start(bf16[64,32,128]{2,1,0:T(8,128)(2,1)} %sum_far.1), calls=%async_computation.2 | async-start | bytes 1048576 | tf_op jit(solution)/shard_map/all_to_all | solution.py:229
  76.0 0.0 copy-done.3
  76.0 0.0 copy-done.5
  76.0 3.5 %outputs.1 = (bf16[1,96,512]{2,1,0:T(8,128)(2,1)}, bf16[1,96,512]{2,1,0:T(8,128)(2,1)}) custom-call(s32[1,512]{1,0:T(1,128)S(1)} %copy-done.3, bf16[27,96,96]{2,1,0:T(8,128)(2,1)S(1)} %copy-done.5, bf16[1056,128]{1,0:T(8,128)(2,1)S(1)} %pack.1.own, bf16[1056,128]{1,0:T(8,128)(2,1)S(1)} %collective-permute-done.before, ...), custom_call_target="tpu_custom_call" | custom-call | flops 905969664 | bytes 2097152 | tf_op jit(solution)/shard_map/outputs/pallas_call | solution.py:204
  79.5 8.8 %all-to-all-done.2.dense = bf16[64,32,128]{2,1,0:T(8,128)(2,1)S(1)} async-done(((bf16[64,32,128]{2,1,0:T(8,128)(2,1)}), bf16[64,32,128]{2,1,0:T(8,128)(2,1)S(1)}, u32[]{:S(2)}, u32[]{:S(2)}) %all-to-all-start.2) | async-done | bytes 524320 | tf_op jit(solution)/shard_map/all_to_all | solution.py:229
  88.3 1.3 %unpack.1 = f32[27,96,96]{2,1,0:T(8,128)} custom-call(bf16[64,32,128]{2,1,0:T(8,128)(2,1)S(1)} %all-to-all-done.2.dense), custom_call_target="tpu_custom_call" | custom-call | bytes 2097152 | tf_op jit(solution)/shard_map/unpack/pallas_call | solution.py:204
  (2 shorter events, 0.0 us)
Async XLA Ops:
  0.6 0.9 copy-start
  1.5 0.9 copy-start.1
  2.4 0.7 copy-start.2
  3.1 0.7 copy-start.4
  4.4 10.7 %collective-permute-start.1 = (bf16[1056,128]{1,0:T(8,128)(2,1)S(1)}, bf16[1056,128]{1,0:T(8,128)(2,1)S(1)}, u32[]{:S(2)}, u32[]{:S(2)}) collective-permute-start(bf16[1056,128]{1,0:T(8,128)(2,1)S(1)} %pack.1.own), channel_id=1, source_target_pairs={{1,0},{2,1},{3,2},{4,3},{5,4},{6,5},{7,6},{8,7},{9,8},{10,9},{11,1... | collective-permute-start | bytes 811016 | tf_op jit(solution)/shard_map/ppermute | solution.py:199
  13.2 5.3 %collective-permute-start = (bf16[1056,128]{1,0:T(8,128)(2,1)S(1)}, bf16[1056,128]{1,0:T(8,128)(2,1)S(1)}, u32[]{:S(2)}, u32[]{:S(2)}) collective-permute-start(bf16[1056,128]{1,0:T(8,128)(2,1)S(1)} %pack.1.own), channel_id=1, source_target_pairs={{0,1},{1,2},{2,3},{3,4},{4,5},{5,6},{6,7},{7,8},{8,9},{9,10},{10,1... | collective-permute-start | bytes 811016 | tf_op jit(solution)/shard_map/ppermute | solution.py:198
  40.8 35.2 %copy-start.3 = (s32[1,512]{1,0:T(1,128)S(1)}, s32[1,512]{1,0:T(1,128)}, u32[]{:S(2)}) copy-start(s32[1,512]{1,0:T(1,128)} %occupancy.5) | copy-start | bytes 6148
  40.8 35.2 %copy-start.5 = (bf16[27,96,96]{2,1,0:T(8,128)(2,1)S(1)}, bf16[27,96,96]{2,1,0:T(8,128)(2,1)}, u32[]{:S(2)}) copy-start(bf16[27,96,96]{2,1,0:T(8,128)(2,1)} %weight.1) | copy-start | bytes 1492996
  69.5 18.8 %all-to-all-start.2 = ((bf16[64,32,128]{2,1,0:T(8,128)(2,1)}), bf16[64,32,128]{2,1,0:T(8,128)(2,1)S(1)}, u32[]{:S(2)}, u32[]{:S(2)}) async-start(bf16[64,32,128]{2,1,0:T(8,128)(2,1)} %sum_far.1), calls=%async_computation.2 | async-start | bytes 1048576 | tf_op jit(solution)/shard_map/all_to_all | solution.py:229

commit v3 on v2

v3 whole, which is shorter than its diff:
```python
import jax
import jax.numpy as jnp
from jax import lax
from jax.experimental import pallas as pl
from jax.experimental.pallas import tpu as pltpu
from jax.sharding import PartitionSpec as P

AXES = ("brick", "chan")
SIGNS = (-1, 0, 1)
VOXELS, LANES, CODES = 512, 128, 32
SHELL = 240
ROWS = 2048
NEAR, FAR = 64, 8
FIRST = 4
OWN, MATE, NEXT, NONE = range(4)
HBM = pl.BlockSpec(memory_space=pltpu.HBM)
VMEM = pl.BlockSpec(memory_space=pltpu.VMEM)
SMEM = pl.BlockSpec(memory_space=pltpu.SMEM)
LIMIT = 32 * 1024 * 1024


def voxel_rows(block):
    spare = jnp.zeros((LANES - block.shape[0], block.shape[1]), jnp.float32)
    return jnp.concatenate([block, spare], axis=0).T


def shell_of(brick):
    pieces = [brick[0], brick[7], brick[1:7, 0], brick[1:7, 7], brick[1:7, :, 0], brick[1:7, :, 7]]
    rows = jnp.concatenate([piece.reshape(-1, LANES) for piece in pieces], axis=0)
    tail = jnp.concatenate([pltpu.roll(rows[SHELL:], 96 - 32 * at, 1) for at in range(3)], axis=0)
    lane = lax.broadcasted_iota(jnp.int32, (SHELL, LANES), 1)
    return jnp.where(lane < 96, rows[:SHELL], tail)


def fill_shell(brick, packed):
    third = SHELL // 3
    lane = lax.broadcasted_iota(jnp.int32, (third, LANES), 1)
    thirds = [pltpu.roll(packed[third * at:third * at + third], 32 + 32 * at, 1) for at in range(3)]
    tail = jnp.where(lane < 32, thirds[0], jnp.where(lane < 64, thirds[1], thirds[2]))
    lane = lax.broadcasted_iota(jnp.int32, (SHELL + third, LANES), 1)
    rows = jnp.where(lane < 96, jnp.concatenate([packed, tail], axis=0), 0.0)
    brick[0] = rows[:64].reshape(8, 8, LANES)
    brick[7] = rows[64:128].reshape(8, 8, LANES)
    brick[1:7, 0] = rows[128:176].reshape(6, 8, LANES)
    brick[1:7, 7] = rows[176:224].reshape(6, 8, LANES)
    brick[1:7, 1:7, 0] = rows[224:272].reshape(6, 8, LANES)[:, 1:7]
    brick[1:7, 1:7, 7] = rows[272:].reshape(6, 8, LANES)[:, 1:7]


def pack_kernel(
    neighbors, occupancy, features, grad_output,
    packed, masked, cotangent_rows, masked_rows, table, flags, inputs, brick, arrived,
):
    copies = [
        pltpu.make_async_copy(source, target, arrived.at[at])
        for at, (source, target) in enumerate((
            (occupancy, flags), (grad_output, inputs.at[0:1]), (features, inputs.at[1:2]), (neighbors, table),
        ))
    ]
    for copy in copies:
        copy.start()
    for copy in copies[:2]:
        copy.wait()
    depth = masked.shape[0]
    occupied = flags[...].astype(jnp.float32)
    for at, rows in ((0, cotangent_rows), (1, masked_rows)):
        if at:
            copies[2].wait()
        product = inputs[at].astype(jnp.float32) * occupied
        if at:
            masked[...] = product.astype(jnp.bfloat16)
        by_voxel = voxel_rows(product)
        rows[...] = by_voxel.astype(jnp.bfloat16)
        brick[at] = by_voxel.reshape(8, 8, 8, LANES)
        packed[SHELL * at:SHELL * (at + 1), :] = shell_of(brick.at[at]).astype(jnp.bfloat16)
    copies[3].wait()
    own = table[0, 13]
    mate = own + 1 - 2 * lax.rem(own, 2)
    row = lax.broadcasted_iota(jnp.int32, (CODES, LANES), 0)
    codes = jnp.full((CODES, LANES), NONE, jnp.int32)
    for offset in range(27):
        brick_id = table[0, offset]
        code = jnp.where(brick_id < 0, NONE, jnp.where(brick_id == own, OWN, jnp.where(brick_id == mate, MATE, NEXT)))
        codes = jnp.where(row == offset, code, codes)
    packed[2 * SHELL:, :] = codes.astype(jnp.float32).astype(jnp.bfloat16)


def faces(sign):
    if sign < 0:
        return slice(7, 8), slice(0, 1)
    if sign > 0:
        return slice(0, 1), slice(9, 10)
    return slice(0, 8), slice(1, 9)


def offset_id(x, y, z):
    return 9 * (x + 1) + 3 * (y + 1) + (z + 1)


def build_windows(bricks, weigh, columns, windows):
    for x in SIGNS:
        from_x, to_x = faces(x)
        for y in SIGNS:
            from_y, to_y = faces(y)
            parts = [brick[from_x, from_y] for brick in bricks]
            shape = parts[0].shape

            def side(z):
                return sum(part * scale for part, scale in zip(parts, weigh(x, y, z)))

            middle = parts[OWN] if x == 0 and y == 0 else side(0)
            middle = middle.reshape(-1, 8, LANES)
            below = side(-1).reshape(-1, 8, LANES)
            above = side(1).reshape(-1, 8, LANES)
            row = lax.broadcasted_iota(jnp.int32, middle.shape, 1)
            columns[0, to_x, to_y] = pltpu.roll(jnp.where(row == 7, below, middle), 1, 1).reshape(shape)
            columns[1, to_x, to_y] = middle.reshape(shape)
            columns[2, to_x, to_y] = pltpu.roll(jnp.where(row == 0, above, middle), 7, 1).reshape(shape)
    for dy in range(3):
        for dz in range(3):
            tap = 3 * dy + dz
            for px in range(10):
                windows[px, :, tap * LANES:(tap + 1) * LANES] = (
                    columns[dz, px, dy:dy + 8].reshape(64, LANES).astype(jnp.bfloat16)
                )


def bricks_of(own, mate, beyond, first, shells):
    shells[...] = jnp.zeros_like(shells)
    for at, ref in enumerate((mate, beyond)):
        fill_shell(shells.at[at], ref[first:first + SHELL, :].astype(jnp.float32))
    return [own[...].astype(jnp.float32).reshape(8, 8, 8, LANES), shells[0], shells[1]]


def codes_of(ref):
    return ref[2 * SHELL:, :].astype(jnp.float32)


def returned_scales(own, mate, beyond):
    tables = [codes_of(ref) for ref in (own, mate, beyond)]

    def weigh(x, y, z):
        at = offset_id(-x, -y, -z)
        return [jnp.where(table[at:at + 1] == code, 1.0, 0.0) for code, table in enumerate(tables)]

    return weigh


def read_scales(own):
    table = codes_of(own)

    def weigh(x, y, z):
        at = offset_id(x, y, z)
        return [jnp.where(table[at:at + 1] == code, 1.0, 0.0) for code in (OWN, MATE, NEXT)]

    return weigh


def span(windows, dx):
    return windows[dx:dx + 8].reshape(VOXELS, 9 * LANES)


def dense_rows(block):
    lane = lax.broadcasted_iota(jnp.int32, (72, LANES), 1)
    tail = jnp.concatenate([pltpu.roll(block[72:], 96 - 32 * third, 1) for third in range(3)], axis=0)
    return jnp.where(lane < 96, block[:72], tail)


def square_rows(dense):
    lane = lax.broadcasted_iota(jnp.int32, (24, LANES), 1)
    thirds = [pltpu.roll(dense[24 * third:24 * third + 24], 32 + 32 * third, 1) for third in range(3)]
    tail = jnp.where(lane < 32, thirds[0], jnp.where(lane < 64, thirds[1], thirds[2]))
    return jnp.concatenate([dense, tail], axis=0)[:, :96]


def weight_grad_kernel(masked, own, mate, beyond, cotangent, grad, columns, windows, shells, dense):
    bricks = bricks_of(cotangent, mate, beyond, 0, shells)
    build_windows(bricks, returned_scales(own, mate, beyond), columns, windows)
    for dx in range(3):
        product = jnp.dot(masked[...], span(windows, dx), preferred_element_type=jnp.float32)
        for tap in range(9):
            at = 72 * (26 - (9 * dx + tap))
            dense[at:at + 72] = dense_rows(product[:, tap * LANES:(tap + 1) * LANES])
    dense[27 * 72:] = jnp.zeros((ROWS - 27 * 72, LANES), jnp.float32)
    grad[...] = dense[...].astype(jnp.bfloat16).reshape(grad.shape)


def sum_kernel(parts, copies):
    total = parts[0].astype(jnp.float32)
    for part in range(1, parts.shape[0]):
        total = total + parts[part].astype(jnp.float32)
    for copy in range(copies.shape[0]):
        copies[copy] = total.astype(copies.dtype)


def unpack_kernel(dense, grad):
    rows = dense[...].reshape(ROWS, LANES).astype(jnp.float32)
    for tap in range(27):
        grad[tap] = square_rows(rows[72 * tap:72 * tap + 72])


def outputs_kernel(
    occupancy, weight, own, mate, beyond, cotangent, masked,
    output, grad_features, columns, windows, shells, taps,
):
    depth = weight.shape[1]
    occupied = occupancy[...].astype(jnp.float32)
    taps[...] = jnp.zeros_like(taps)
    for tap in range(27):
        taps[tap, :depth, :depth] = weight[tap]

    def finish(rows):
        return (rows.T[:depth] * occupied).astype(jnp.bfloat16)

    bricks = bricks_of(masked, mate, beyond, SHELL, shells)
    build_windows(bricks, read_scales(own), columns, windows)
    total = jnp.zeros((VOXELS, LANES), jnp.float32)
    for dx in range(3):
        kernel = taps[9 * dx:9 * dx + 9].reshape(9 * LANES, LANES)
        total = total + jnp.dot(span(windows, dx), kernel, preferred_element_type=jnp.float32)
    output[0] = finish(total)

    bricks = bricks_of(cotangent, mate, beyond, 0, shells)
    build_windows(bricks, returned_scales(own, mate, beyond), columns, windows)
    total = jnp.zeros((VOXELS, LANES), jnp.float32)
    for dx in range(3):
        for tap in range(9):
            total = total + lax.dot_general(
                windows[dx:dx + 8, :, tap * LANES:(tap + 1) * LANES].reshape(VOXELS, LANES),
                taps[26 - (9 * dx + tap)],
                (((1,), (1,)), ((), ())),
                preferred_element_type=jnp.float32,
            )
    grad_features[0] = finish(total)


WINDOW_SCRATCH = [
    pltpu.VMEM((3, 10, 10, 8, LANES), jnp.float32),
    pltpu.VMEM((10, 64, 9 * LANES), jnp.bfloat16),
    pltpu.VMEM((2, 8, 8, 8, LANES), jnp.float32),
]


def neighbours(block):
    count = lax.axis_size("brick") * lax.axis_size("chan")
    beyond = lax.ppermute(block, AXES, [(i, i + 2 * (i % 2) - 1) for i in range(1, count - 1)])
    mate = lax.ppermute(block, AXES, [(i, i + 1 - 2 * (i % 2)) for i in range(count)])
    return mate, beyond


def call(kernel, name, shapes, operands, specs=None, scratch=(), flops=0, limit=LIMIT):
    return pl.pallas_call(
        kernel,
        out_shape=shapes,
        in_specs=specs or [VMEM] * len(operands),
        out_specs=jax.tree.map(lambda _: VMEM, shapes),
        scratch_shapes=list(scratch),
        compiler_params=pltpu.CompilerParams(vmem_limit_bytes=limit),
        cost_estimate=pl.CostEstimate(flops=flops, bytes_accessed=2 * 1024 * 1024, transcendentals=0),
        name=name,
    )(*operands)


def bf16(*shape):
    return jax.ShapeDtypeStruct(shape, jnp.bfloat16)


def total_over_devices(grad):
    rows = grad.shape[1]
    count = NEAR * FAR
    near = [[first + i for i in range(NEAR)] for first in range(0, count, NEAR)]
    far = [[first + NEAR * ((i + FIRST) % FAR) for i in range(FAR)] for first in range(NEAR)]
    pieces = lax.all_to_all(grad, AXES, 0, 0, tiled=True, axis_index_groups=near)
    share = call(sum_kernel, "sum_near", bf16(FAR, rows, LANES), (pieces,))
    shares = lax.all_to_all(share, AXES, 0, 0, tiled=True, axis_index_groups=far)
    whole = call(sum_kernel, "sum_far", bf16(NEAR, rows, LANES), (shares,))
    return lax.all_to_all(whole, AXES, 0, 0, tiled=True, axis_index_groups=near)


def shards(features, occupancy, neighbors, weight, grad_output):
    depth = features.shape[1]
    own, masked, cotangent_rows, masked_rows = call(
        pack_kernel, "pack",
        [bf16(2 * SHELL + CODES, LANES), bf16(depth, VOXELS), bf16(VOXELS, LANES), bf16(VOXELS, LANES)],
        (neighbors, occupancy, features, grad_output), [HBM] * 4,
        scratch=[
            pltpu.SMEM(neighbors.shape, jnp.int32),
            pltpu.VMEM(occupancy.shape, jnp.int32),
            pltpu.VMEM((2, depth, VOXELS), jnp.bfloat16),
            pltpu.VMEM((2, 8, 8, 8, LANES), jnp.float32),
            pltpu.SemaphoreType.DMA((4,)),
        ],
    )
    mate, beyond = neighbours(own)
    dot = 27 * 2 * LANES * LANES * VOXELS
    grad = call(
        weight_grad_kernel, "weight_grad", bf16(NEAR, ROWS // NEAR, LANES),
        (masked, own, mate, beyond, cotangent_rows),
        scratch=WINDOW_SCRATCH + [pltpu.VMEM((ROWS, LANES), jnp.float32)], flops=dot,
    )
    grad = total_over_devices(grad)
    output, grad_features = call(
        outputs_kernel, "outputs", [bf16(*features.shape)] * 2,
        (occupancy, weight, own, mate, beyond, cotangent_rows, masked_rows),
        scratch=WINDOW_SCRATCH + [pltpu.VMEM((27, LANES, LANES), jnp.bfloat16)], flops=2 * dot,
    )
    grad_weight = call(unpack_kernel, "unpack", jax.ShapeDtypeStruct((27, depth, depth), jnp.float32), (grad,))
    return output, grad_features, grad_weight


def solution(mesh):
    split = P(AXES, None, None)
    flat = P(AXES, None)
    return jax.shard_map(
        shards,
        mesh=mesh,
        in_specs=(split, flat, flat, P(), split),
        out_specs=(split, split, P()),
        check_vma=False,
    )
```

time: 90 us -> 77.8 us (0.86)
  blocking collectives: 49 us -> 40.6 us
  waiting for transfers between devices: 12.2 us -> 9.41 us
  starting transfers between devices: 17.2 us -> 15.7 us
    all_to_all x1, blocking collectives: 27.8 us -> 19.2 us  [total_over_devices(): lax.all_to_all(share, AXES, 0, 0, tiled=True, axis_index_groups=far)]
    ppermute x2, waiting for transfers between devices: 3.37 us -> 0.96 us  [the longest x1 0.95 us: neighbours(): lax.ppermute(block, AXES, [(i, i + 1 - 2 * (i % 2)) for i in range(count)])]
    ppermute x2, starting transfers between devices: 10.7 us -> 9.46 us  [the longest x1 4.86 us: neighbours(): lax.ppermute(block, AXES, [(i, i + 1 - 2 * (i % 2)) for i in range(count)])]
  transfers between devices with their start and end apart: 3 -> 3, of which waited for: 2 -> 2; matrix products, arithmetic and copies ran while one was open for 0% -> 0% of each run, Pallas kernels for 4% -> 5%
where the time goes in v3:
time: 77.8 us; the launch traced here: 77.5 us
  blocking collectives  40.6 us (52%)
  starting transfers between devices  15.7 us (20%)
  waiting for transfers between devices  9.41 us (12%)
  Pallas kernels  7.88 us (10%)
  local copies, waits for them, and re-layouts  3.12 us (4%)
    all_to_all x1, blocking collectives, total_over_devices(): lax.all_to_all(grad, AXES, 0, 0, tiled=True, axis_index_groups=near)  21.4 us
    all_to_all x1, blocking collectives, total_over_devices(): lax.all_to_all(share, AXES, 0, 0, tiled=True, axis_index_groups=far)  19.2 us
    all_to_all x1, waiting for transfers between devices, total_over_devices(): return lax.all_to_all(whole, AXES, 0, 0, tiled=True, axis_index_groups=near)  8.46 us
    pallas_call x6, Pallas kernels, call(): pl.pallas_call(kernel, out_shape=shapes, in_specs=specs or [VMEM] * len(o...  7.88 us
    all_to_all x1, starting transfers between devices, total_over_devices(): return lax.all_to_all(whole, AXES, 0, 0, tiled=True, axis_index_groups=near)  6.28 us
    ppermute x1, starting transfers between devices, neighbours(): lax.ppermute(block, AXES, [(i, i + 1 - 2 * (i % 2)) for i in range(count)])  4.86 us
    ppermute x1, starting transfers between devices, neighbours(): lax.ppermute(block, AXES, [(i, i + 2 * (i % 2) - 1) for i in range(1, cou...  4.59 us
    unnamed x12, local copies, waits for them, and re-layouts  3.12 us
  transfers between devices with their start and end apart: 3, of which 2 were waited for; matrix products, arithmetic and copies ran while one was open for 0% of the time, Pallas kernels for 5%

profile of v3, /device:TPU:1, one launch (start us, length us, event | category | flops | bytes accessed | tf_op | source)
XLA Modules:
  0.0 77.5 jit_solution(3547562866104305928)
XLA Ops:
  0.6 0.0 copy-start
  0.6 0.9 %copy-done = bf16[1,96,512]{2,1,0:T(8,128)(2,1)S(1)} copy-done((bf16[1,96,512]{2,1,0:T(8,128)(2,1)S(1)}, bf16[1,96,512]{2,1,0:T(8,128)(2,1)}, u32[]{:S(2)}) %copy-start) | copy-done | bytes 98328
  1.5 0.0 copy-start.1
  1.5 0.9 %copy-done.1 = bf16[1,96,512]{2,1,0:T(8,128)(2,1)S(1)} copy-done((bf16[1,96,512]{2,1,0:T(8,128)(2,1)S(1)}, bf16[1,96,512]{2,1,0:T(8,128)(2,1)}, u32[]{:S(2)}) %copy-start.1) | copy-done | bytes 98328
  2.4 0.0 copy-start.2
  2.4 0.7 copy-done.2
  3.1 0.0 copy-start.4
  3.1 0.7 copy-done.4
  3.8 0.9 %pack.1 = (bf16[512,128]{1,0:T(8,128)(2,1)S(1)}, bf16[96,512]{1,0:T(8,128)(2,1)S(1)}, bf16[512,128]{1,0:T(8,128)(2,1)S(1)}, bf16[512,128]{1,0:T(8,128)(2,1)S(1)}) custom-call(s32[1,27]{1,0:T(1,128)S(1)} %copy-done.4, s32[1,512]{1,0:T(1,128)S(1)} %copy-done.2, bf16[1,96,512]{2,1,0:T(8,128)(2,1)S(1)} %copy-done, bf16[1,96,512]{2,1,0:T(8,128)(2,1)S(1)} %copy-done.1), custom_call_target="tpu_custom_call" | custom-call | bytes 2097152 | tf_op jit(solution)/shard_map/pack/pallas_call | solution.py:252
  4.6 4.6 %collective-permute-start.1 = (bf16[512,128]{1,0:T(8,128)(2,1)S(1)}, bf16[512,128]{1,0:T(8,128)(2,1)S(1)}, u32[]{:S(2)}, u32[]{:S(2)}) collective-permute-start(bf16[512,128]{1,0:T(8,128)(2,1)S(1)} %get-tuple-element.9.own), channel_id=1, source_target_pairs={{1,2},{2,1},{3,4},{4,3},{5,6},{6,5},{7,8},{8,7},{9,10},{10,9},{11,... | collective-permute-start | bytes 393224 | tf_op jit(solution)/shard_map/ppermute | solution.py:246
  9.2 4.9 %collective-permute-start = (bf16[512,128]{1,0:T(8,128)(2,1)S(1)}, bf16[512,128]{1,0:T(8,128)(2,1)S(1)}, u32[]{:S(2)}, u32[]{:S(2)}) collective-permute-start(bf16[512,128]{1,0:T(8,128)(2,1)S(1)} %get-tuple-element.9.own), channel_id=1, source_target_pairs={{0,1},{1,0},{2,3},{3,2},{4,5},{5,4},{6,7},{7,6},{8,9},{9,8},{10,11... | collective-permute-start | bytes 393224 | tf_op jit(solution)/shard_map/ppermute | solution.py:247
  14.1 0.0 collective-permute-done.1.beyond
  14.1 1.0 %collective-permute-done.mate = bf16[512,128]{1,0:T(8,128)(2,1)S(1)} collective-permute-done((bf16[512,128]{1,0:T(8,128)(2,1)S(1)}, bf16[512,128]{1,0:T(8,128)(2,1)S(1)}, u32[]{:S(2)}, u32[]{:S(2)}) %collective-permute-start) | collective-permute-done | bytes 131104 | tf_op jit(solution)/shard_map/ppermute | solution.py:247
  15.1 1.1 %weight_grad.1 = bf16[64,32,128]{2,1,0:T(8,128)(2,1)S(1)} custom-call(bf16[96,512]{1,0:T(8,128)(2,1)S(1)} %get-tuple-element.14.masked, bf16[512,128]{1,0:T(8,128)(2,1)S(1)} %get-tuple-element.9.own, bf16[512,128]{1,0:T(8,128)(2,1)S(1)} %collective-permute-done.mate, bf16[512,128]{1,0:T(8,128)(2,1)S(1)} %collective-permute-done.1.beyond, ...), custom_call_target="tpu_custom_call" | custom-call | flops 452984832 | bytes 2097152 | tf_op jit(solution)/shard_map/weight_grad/pallas_call | solution.py:252
  16.2 21.4 %all_to_all.15.parts = bf16[64,32,128]{2,1,0:T(8,128)(2,1)S(1)} all-to-all(bf16[64,32,128]{2,1,0:T(8,128)(2,1)S(1)} %weight_grad.1), channel_id=1, replica_groups={{0,1,2,3,4,5,6,7,8,9,10,11,12,13,14,15,16,17,18,19,20,21,22,23,24,25,26..., dimensions={0} | all-to-all | bytes 1048576 | tf_op jit(solution)/shard_map/all_to_all | solution.py:273
  37.6 0.1 sum_near.1
  37.7 19.2 %all_to_all.16.parts = bf16[8,32,128]{2,1,0:T(8,128)(2,1)S(1)} all-to-all(bf16[8,32,128]{2,1,0:T(8,128)(2,1)S(1)} %sum_near.1), channel_id=1, replica_groups={{256,320,384,448,0,64,128,192},{257,321,385,449,1,65,129,193},{258,322,..., dimensions={0} | all-to-all | bytes 131072 | tf_op jit(solution)/shard_map/all_to_all | solution.py:275
  56.9 0.8 %sum_far.1 = bf16[64,32,128]{2,1,0:T(8,128)(2,1)} custom-call(bf16[8,32,128]{2,1,0:T(8,128)(2,1)S(1)} %all_to_all.16.parts), custom_call_target="tpu_custom_call" | custom-call | bytes 2097152 | tf_op jit(solution)/shard_map/sum_far/pallas_call | solution.py:252
  57.7 6.3 %all-to-all-start.2 = ((bf16[64,32,128]{2,1,0:T(8,128)(2,1)}), bf16[64,32,128]{2,1,0:T(8,128)(2,1)S(1)}, u32[]{:S(2)}, u32[]{:S(2)}) async-start(bf16[64,32,128]{2,1,0:T(8,128)(2,1)} %sum_far.1), calls=%async_computation.2 | async-start | bytes 1048576 | tf_op jit(solution)/shard_map/all_to_all | solution.py:277
  64.0 0.0 copy-done.3
  64.0 0.0 copy-done.5
  64.0 3.7 %outputs.1 = (bf16[1,96,512]{2,1,0:T(8,128)(2,1)}, bf16[1,96,512]{2,1,0:T(8,128)(2,1)}) custom-call(s32[1,512]{1,0:T(1,128)S(1)} %copy-done.3, bf16[27,96,96]{2,1,0:T(8,128)(2,1)S(1)} %copy-done.5, bf16[512,128]{1,0:T(8,128)(2,1)S(1)} %get-tuple-element.9.own, bf16[512,128]{1,0:T(8,128)(2,1)S(1)} %collective-permute-done.mate, ...), custom_call_target="tpu_custom_call" | custom-call | flops 905969664 | bytes 2097152 | tf_op jit(solution)/shard_map/outputs/pallas_call | solution.py:252
  67.7 8.5 %all-to-all-done.2.dense = bf16[64,32,128]{2,1,0:T(8,128)(2,1)S(1)} async-done(((bf16[64,32,128]{2,1,0:T(8,128)(2,1)}), bf16[64,32,128]{2,1,0:T(8,128)(2,1)S(1)}, u32[]{:S(2)}, u32[]{:S(2)}) %all-to-all-start.2) | async-done | bytes 524320 | tf_op jit(solution)/shard_map/all_to_all | solution.py:277
  76.2 1.3 %unpack.1 = f32[27,96,96]{2,1,0:T(8,128)} custom-call(bf16[64,32,128]{2,1,0:T(8,128)(2,1)S(1)} %all-to-all-done.2.dense), custom_call_target="tpu_custom_call" | custom-call | bytes 2097152 | tf_op jit(solution)/shard_map/unpack/pallas_call | solution.py:252
  (2 shorter events, 0.0 us)
Async XLA Ops:
  0.6 0.9 %copy-start = (bf16[1,96,512]{2,1,0:T(8,128)(2,1)S(1)}, bf16[1,96,512]{2,1,0:T(8,128)(2,1)}, u32[]{:S(2)}) copy-start(bf16[1,96,512]{2,1,0:T(8,128)(2,1)} %features.1) | copy-start | bytes 294916
  1.5 0.9 %copy-start.1 = (bf16[1,96,512]{2,1,0:T(8,128)(2,1)S(1)}, bf16[1,96,512]{2,1,0:T(8,128)(2,1)}, u32[]{:S(2)}) copy-start(bf16[1,96,512]{2,1,0:T(8,128)(2,1)} %grad_output.1) | copy-start | bytes 294916
  2.4 0.7 copy-start.2
  3.1 0.7 copy-start.4
  4.6 9.5 %collective-permute-start.1 = (bf16[512,128]{1,0:T(8,128)(2,1)S(1)}, bf16[512,128]{1,0:T(8,128)(2,1)S(1)}, u32[]{:S(2)}, u32[]{:S(2)}) collective-permute-start(bf16[512,128]{1,0:T(8,128)(2,1)S(1)} %get-tuple-element.9.own), channel_id=1, source_target_pairs={{1,2},{2,1},{3,4},{4,3},{5,6},{6,5},{7,8},{8,7},{9,10},{10,9},{11,... | collective-permute-start | bytes 393224 | tf_op jit(solution)/shard_map/ppermute | solution.py:246
  9.2 5.8 %collective-permute-start = (bf16[512,128]{1,0:T(8,128)(2,1)S(1)}, bf16[512,128]{1,0:T(8,128)(2,1)S(1)}, u32[]{:S(2)}, u32[]{:S(2)}) collective-permute-start(bf16[512,128]{1,0:T(8,128)(2,1)S(1)} %get-tuple-element.9.own), channel_id=1, source_target_pairs={{0,1},{1,0},{2,3},{3,2},{4,5},{5,4},{6,7},{7,6},{8,9},{9,8},{10,11... | collective-permute-start | bytes 393224 | tf_op jit(solution)/shard_map/ppermute | solution.py:247
  37.6 26.4 %copy-start.3 = (s32[1,512]{1,0:T(1,128)S(1)}, s32[1,512]{1,0:T(1,128)}, u32[]{:S(2)}) copy-start(s32[1,512]{1,0:T(1,128)} %occupancy.3) | copy-start | bytes 6148
  37.6 26.4 %copy-start.5 = (bf16[27,96,96]{2,1,0:T(8,128)(2,1)S(1)}, bf16[27,96,96]{2,1,0:T(8,128)(2,1)}, u32[]{:S(2)}) copy-start(bf16[27,96,96]{2,1,0:T(8,128)(2,1)} %weight.1) | copy-start | bytes 1492996
  57.7 18.5 %all-to-all-start.2 = ((bf16[64,32,128]{2,1,0:T(8,128)(2,1)}), bf16[64,32,128]{2,1,0:T(8,128)(2,1)S(1)}, u32[]{:S(2)}, u32[]{:S(2)}) async-start(bf16[64,32,128]{2,1,0:T(8,128)(2,1)} %sum_far.1), calls=%async_computation.2 | async-start | bytes 1048576 | tf_op jit(solution)/shard_map/all_to_all | solution.py:277

commit v4 on v3

--- a/solution.py
+++ b/solution.py
@@ -11,11 +11,11 @@
 SHELL = 240
 ROWS = 2048
 NEAR, FAR = 64, 8
+SCATTER = [(13 * i + 63) % NEAR for i in range(NEAR)]
+GATHER = SCATTER
 FIRST = 4
 OWN, MATE, NEXT, NONE = range(4)
-HBM = pl.BlockSpec(memory_space=pltpu.HBM)
 VMEM = pl.BlockSpec(memory_space=pltpu.VMEM)
-SMEM = pl.BlockSpec(memory_space=pltpu.SMEM)
 LIMIT = 32 * 1024 * 1024
 
 
@@ -47,42 +47,22 @@
     brick[1:7, 1:7, 7] = rows[272:].reshape(6, 8, LANES)[:, 1:7]
 
 
-def pack_kernel(
-    neighbors, occupancy, features, grad_output,
-    packed, masked, cotangent_rows, masked_rows, table, flags, inputs, brick, arrived,
-):
-    copies = [
-        pltpu.make_async_copy(source, target, arrived.at[at])
-        for at, (source, target) in enumerate((
-            (occupancy, flags), (grad_output, inputs.at[0:1]), (features, inputs.at[1:2]), (neighbors, table),
-        ))
-    ]
-    for copy in copies:
-        copy.start()
-    for copy in copies[:2]:
-        copy.wait()
-    depth = masked.shape[0]
-    occupied = flags[...].astype(jnp.float32)
+def pack_kernel(pair, side, packed, masked, cotangent_rows, masked_rows, brick):
+    occupied = side[0:1, :VOXELS].astype(jnp.float32)
     for at, rows in ((0, cotangent_rows), (1, masked_rows)):
-        if at:
-            copies[2].wait()
-        product = inputs[at].astype(jnp.float32) * occupied
+        product = pair[at].astype(jnp.float32) * occupied
         if at:
             masked[...] = product.astype(jnp.bfloat16)
         by_voxel = voxel_rows(product)
         rows[...] = by_voxel.astype(jnp.bfloat16)
         brick[at] = by_voxel.reshape(8, 8, 8, LANES)
         packed[SHELL * at:SHELL * (at + 1), :] = shell_of(brick.at[at]).astype(jnp.bfloat16)
-    copies[3].wait()
-    own = table[0, 13]
-    mate = own + 1 - 2 * lax.rem(own, 2)
-    row = lax.broadcasted_iota(jnp.int32, (CODES, LANES), 0)
-    codes = jnp.full((CODES, LANES), NONE, jnp.int32)
-    for offset in range(27):
-        brick_id = table[0, offset]
-        code = jnp.where(brick_id < 0, NONE, jnp.where(brick_id == own, OWN, jnp.where(brick_id == mate, MATE, NEXT)))
-        codes = jnp.where(row == offset, code, codes)
-    packed[2 * SHELL:, :] = codes.astype(jnp.float32).astype(jnp.bfloat16)
+    bricks = side[0:1, VOXELS:VOXELS + LANES]
+    lane = lax.broadcasted_iota(jnp.int32, (1, LANES), 1)
+    own = jnp.sum(jnp.where(lane == 13, bricks, 0), axis=1, keepdims=True)
+    codes = jnp.where(bricks == own, OWN, jnp.where(bricks == (own ^ 1), MATE, NEXT))
+    codes = jnp.where(bricks < 0, NONE, codes).astype(jnp.float32)
+    packed[2 * SHELL:, :] = jnp.broadcast_to(codes, (LANES, LANES)).T[:CODES].astype(jnp.bfloat16)
 
 
 def faces(sign):
@@ -194,7 +174,8 @@
 
 
 def unpack_kernel(dense, grad):
-    rows = dense[...].reshape(ROWS, LANES).astype(jnp.float32)
+    shares = [dense[GATHER.index(member)] for member in SCATTER]
+    rows = jnp.concatenate(shares, axis=0).astype(jnp.float32)
     for tap in range(27):
         grad[tap] = square_rows(rows[72 * tap:72 * tap + 72])
 
@@ -265,31 +246,29 @@
     return jax.ShapeDtypeStruct(shape, jnp.bfloat16)
 
 
+def near_groups(order):
+    count = NEAR * FAR
+    return [[first + member for member in order] for first in range(0, count, NEAR)]
+
+
 def total_over_devices(grad):
     rows = grad.shape[1]
-    count = NEAR * FAR
-    near = [[first + i for i in range(NEAR)] for first in range(0, count, NEAR)]
     far = [[first + NEAR * ((i + FIRST) % FAR) for i in range(FAR)] for first in range(NEAR)]
-    pieces = lax.all_to_all(grad, AXES, 0, 0, tiled=True, axis_index_groups=near)
+    pieces = lax.all_to_all(grad, AXES, 0, 0, tiled=True, axis_index_groups=near_groups(SCATTER))
     share = call(sum_kernel, "sum_near", bf16(FAR, rows, LANES), (pieces,))
     shares = lax.all_to_all(share, AXES, 0, 0, tiled=True, axis_index_groups=far)
     whole = call(sum_kernel, "sum_far", bf16(NEAR, rows, LANES), (shares,))
-    return lax.all_to_all(whole, AXES, 0, 0, tiled=True, axis_index_groups=near)
+    return lax.all_to_all(whole, AXES, 0, 0, tiled=True, axis_index_groups=near_groups(GATHER))
 
 
 def shards(features, occupancy, neighbors, weight, grad_output):
     depth = features.shape[1]
+    pair = jnp.concatenate([grad_output, features])
+    side = jnp.pad(neighbors, ((0, 0), (VOXELS, LANES - 27))) + jnp.pad(occupancy, ((0, 0), (0, LANES)))
     own, masked, cotangent_rows, masked_rows = call(
         pack_kernel, "pack",
         [bf16(2 * SHELL + CODES, LANES), bf16(depth, VOXELS), bf16(VOXELS, LANES), bf16(VOXELS, LANES)],
-        (neighbors, occupancy, features, grad_output), [HBM] * 4,
-        scratch=[
-            pltpu.SMEM(neighbors.shape, jnp.int32),
-            pltpu.VMEM(occupancy.shape, jnp.int32),
-            pltpu.VMEM((2, depth, VOXELS), jnp.bfloat16),
-            pltpu.VMEM((2, 8, 8, 8, LANES), jnp.float32),
-            pltpu.SemaphoreType.DMA((4,)),
-        ],
+        (pair, side), scratch=[pltpu.VMEM((2, 8, 8, 8, LANES), jnp.float32)],
     )
     mate, beyond = neighbours(own)
     dot = 27 * 2 * LANES * LANES * VOXELS

time: 77.8 us -> 72.7 us (0.934)
  waiting for transfers between devices: 9.41 us -> 5.47 us
  starting transfers between devices: 15.7 us -> 19.2 us
  local copies, waits for them, and re-layouts: 3.12 us -> 0.01 us
  blocking collectives: 40.6 us -> 37.9 us
  other arithmetic: 0 us -> 1.65 us
    all_to_all x1, waiting for transfers between devices: 8.46 us -> 4.51 us  [total_over_devices(): lax.all_to_all(whole, AXES, 0, 0, tiled=True, axis_index_groups=near_grou...]
    all_to_all x1, starting transfers between devices: 6.28 us -> 9.77 us  [total_over_devices(): lax.all_to_all(whole, AXES, 0, 0, tiled=True, axis_index_groups=near_grou...]
    unnamed x12 -> x4, local copies, waits for them, and re-layouts: 3.12 us -> 0.01 us
    all_to_all x1, blocking collectives: 21.4 us -> 18.8 us  [total_over_devices(): lax.all_to_all(grad, AXES, 0, 0, tiled=True, axis_index_groups=near_group...]
    concatenate x0 -> x1, other arithmetic: none -> 0.96 us  [shards(): pair = jnp.concatenate([grad_output, features])]
where the time goes in v4:
time: 72.7 us; the launch traced here: 72.4 us
  blocking collectives  37.9 us (52%)
  starting transfers between devices  19.2 us (26%)
  Pallas kernels  7.4 us (10%)
  waiting for transfers between devices  5.47 us (8%)
  other arithmetic  1.65 us (2%)
    all_to_all x1, blocking collectives, total_over_devices(): lax.all_to_all(share, AXES, 0, 0, tiled=True, axis_index_groups=far)  19.1 us
    all_to_all x1, blocking collectives, total_over_devices(): lax.all_to_all(grad, AXES, 0, 0, tiled=True, axis_index_groups=near_group...  18.8 us
    all_to_all x1, starting transfers between devices, total_over_devices(): lax.all_to_all(whole, AXES, 0, 0, tiled=True, axis_index_groups=near_grou...  9.77 us
    pallas_call x6, Pallas kernels, call(): pl.pallas_call(kernel, out_shape=shapes, in_specs=specs or [VMEM] * len(o...  7.4 us
    ppermute x1, starting transfers between devices, neighbours(): lax.ppermute(block, AXES, [(i, i + 1 - 2 * (i % 2)) for i in range(count)])  4.86 us
    ppermute x1, starting transfers between devices, neighbours(): lax.ppermute(block, AXES, [(i, i + 2 * (i % 2) - 1) for i in range(1, cou...  4.59 us
    all_to_all x1, waiting for transfers between devices, total_over_devices(): lax.all_to_all(whole, AXES, 0, 0, tiled=True, axis_index_groups=near_grou...  4.51 us
  transfers between devices with their start and end apart: 3, of which 2 were waited for; matrix products, arithmetic and copies ran while one was open for 0% of the time, Pallas kernels for 5%

profile of v4, /device:TPU:1, one launch (start us, length us, event | category | flops | bytes accessed | tf_op | source)
XLA Modules:
  0.0 72.4 jit_solution(10731949552342061913)
XLA Ops:
  0.6 0.7 pad_add_fusion.side
  1.3 1.0 %pad_maximum_fusion.pair = bf16[2,96,512]{2,1,0:T(8,128)(2,1)S(1)} fusion(bf16[1,96,512]{2,1,0:T(8,128)(2,1)} %param.5, bf16[1,96,512]{2,1,0:T(8,128)(2,1)} %param.9), kind=kLoop, calls=%fused_computation | loop fusion | flops 98304 | bytes 393216 | tf_op jit(solution)/shard_map/concatenate | solution.py:266
  2.3 0.4 pack.1
  2.7 4.6 %collective-permute-start.1 = (bf16[512,128]{1,0:T(8,128)(2,1)S(1)}, bf16[512,128]{1,0:T(8,128)(2,1)S(1)}, u32[]{:S(2)}, u32[]{:S(2)}) collective-permute-start(bf16[512,128]{1,0:T(8,128)(2,1)S(1)} %get-tuple-element.9.own), channel_id=1, source_target_pairs={{1,2},{2,1},{3,4},{4,3},{5,6},{6,5},{7,8},{8,7},{9,10},{10,9},{11,... | collective-permute-start | bytes 393224 | tf_op jit(solution)/shard_map/ppermute | solution.py:227
  7.3 4.9 %collective-permute-start = (bf16[512,128]{1,0:T(8,128)(2,1)S(1)}, bf16[512,128]{1,0:T(8,128)(2,1)S(1)}, u32[]{:S(2)}, u32[]{:S(2)}) collective-permute-start(bf16[512,128]{1,0:T(8,128)(2,1)S(1)} %get-tuple-element.9.own), channel_id=1, source_target_pairs={{0,1},{1,0},{2,3},{3,2},{4,5},{5,4},{6,7},{7,6},{8,9},{9,8},{10,11... | collective-permute-start | bytes 393224 | tf_op jit(solution)/shard_map/ppermute | solution.py:228
  12.1 0.0 collective-permute-done.1.beyond
  12.1 1.0 %collective-permute-done.mate = bf16[512,128]{1,0:T(8,128)(2,1)S(1)} collective-permute-done((bf16[512,128]{1,0:T(8,128)(2,1)S(1)}, bf16[512,128]{1,0:T(8,128)(2,1)S(1)}, u32[]{:S(2)}, u32[]{:S(2)}) %collective-permute-start) | collective-permute-done | bytes 131104 | tf_op jit(solution)/shard_map/ppermute | solution.py:228
  13.1 1.1 %weight_grad.1 = bf16[64,32,128]{2,1,0:T(8,128)(2,1)S(1)} custom-call(bf16[96,512]{1,0:T(8,128)(2,1)S(1)} %get-tuple-element.14.masked, bf16[512,128]{1,0:T(8,128)(2,1)S(1)} %get-tuple-element.9.own, bf16[512,128]{1,0:T(8,128)(2,1)S(1)} %collective-permute-done.mate, bf16[512,128]{1,0:T(8,128)(2,1)S(1)} %collective-permute-done.1.beyond, ...), custom_call_target="tpu_custom_call" | custom-call | flops 452984832 | bytes 2097152 | tf_op jit(solution)/shard_map/weight_grad/pallas_call | solution.py:233
  14.2 18.8 %all_to_all.15.parts = bf16[64,32,128]{2,1,0:T(8,128)(2,1)S(1)} all-to-all(bf16[64,32,128]{2,1,0:T(8,128)(2,1)S(1)} %weight_grad.1), channel_id=1, replica_groups={{63,12,25,38,51,0,13,26,39,52,1,14,27,40,53,2,15,28,41,54,3,16,29,42,55..., dimensions={0} | all-to-all | bytes 1048576 | tf_op jit(solution)/shard_map/all_to_all | solution.py:257
  33.0 0.0 copy-start
  33.0 0.0 copy-start.1
  33.0 0.1 sum_near.1
  33.1 19.1 %all_to_all.16.parts = bf16[8,32,128]{2,1,0:T(8,128)(2,1)S(1)} all-to-all(bf16[8,32,128]{2,1,0:T(8,128)(2,1)S(1)} %sum_near.1), channel_id=1, replica_groups={{256,320,384,448,0,64,128,192},{257,321,385,449,1,65,129,193},{258,322,..., dimensions={0} | all-to-all | bytes 131072 | tf_op jit(solution)/shard_map/all_to_all | solution.py:259
  52.2 0.8 %sum_far.1 = bf16[64,32,128]{2,1,0:T(8,128)(2,1)} custom-call(bf16[8,32,128]{2,1,0:T(8,128)(2,1)S(1)} %all_to_all.16.parts), custom_call_target="tpu_custom_call" | custom-call | bytes 2097152 | tf_op jit(solution)/shard_map/sum_far/pallas_call | solution.py:233
  53.1 9.8 %all-to-all-start.2 = ((bf16[64,32,128]{2,1,0:T(8,128)(2,1)}), bf16[64,32,128]{2,1,0:T(8,128)(2,1)S(1)}, u32[]{:S(2)}, u32[]{:S(2)}) async-start(bf16[64,32,128]{2,1,0:T(8,128)(2,1)} %sum_far.1), calls=%async_computation.2 | async-start | bytes 1048576 | tf_op jit(solution)/shard_map/all_to_all | solution.py:261
  62.9 0.0 copy-done
  62.9 0.0 copy-done.1
  62.9 3.7 %outputs.1 = (bf16[1,96,512]{2,1,0:T(8,128)(2,1)}, bf16[1,96,512]{2,1,0:T(8,128)(2,1)}) custom-call(s32[1,512]{1,0:T(1,128)S(1)} %copy-done, bf16[27,96,96]{2,1,0:T(8,128)(2,1)S(1)} %copy-done.1, bf16[512,128]{1,0:T(8,128)(2,1)S(1)} %get-tuple-element.9.own, bf16[512,128]{1,0:T(8,128)(2,1)S(1)} %collective-permute-done.mate, ...), custom_call_target="tpu_custom_call" | custom-call | flops 905969664 | bytes 2097152 | tf_op jit(solution)/shard_map/outputs/pallas_call | solution.py:233
  66.6 4.5 %all-to-all-done.2.dense = bf16[64,32,128]{2,1,0:T(8,128)(2,1)S(1)} async-done(((bf16[64,32,128]{2,1,0:T(8,128)(2,1)}), bf16[64,32,128]{2,1,0:T(8,128)(2,1)S(1)}, u32[]{:S(2)}, u32[]{:S(2)}) %all-to-all-start.2) | async-done | bytes 524320 | tf_op jit(solution)/shard_map/all_to_all | solution.py:261
  71.1 1.3 %unpack.1 = f32[27,96,96]{2,1,0:T(8,128)} custom-call(bf16[64,32,128]{2,1,0:T(8,128)(2,1)S(1)} %all-to-all-done.2.dense), custom_call_target="tpu_custom_call" | custom-call | bytes 2097152 | tf_op jit(solution)/shard_map/unpack/pallas_call | solution.py:233
Async XLA Ops:
  2.7 9.5 %collective-permute-start.1 = (bf16[512,128]{1,0:T(8,128)(2,1)S(1)}, bf16[512,128]{1,0:T(8,128)(2,1)S(1)}, u32[]{:S(2)}, u32[]{:S(2)}) collective-permute-start(bf16[512,128]{1,0:T(8,128)(2,1)S(1)} %get-tuple-element.9.own), channel_id=1, source_target_pairs={{1,2},{2,1},{3,4},{4,3},{5,6},{6,5},{7,8},{8,7},{9,10},{10,9},{11,... | collective-permute-start | bytes 393224 | tf_op jit(solution)/shard_map/ppermute | solution.py:227
  7.3 5.8 %collective-permute-start = (bf16[512,128]{1,0:T(8,128)(2,1)S(1)}, bf16[512,128]{1,0:T(8,128)(2,1)S(1)}, u32[]{:S(2)}, u32[]{:S(2)}) collective-permute-start(bf16[512,128]{1,0:T(8,128)(2,1)S(1)} %get-tuple-element.9.own), channel_id=1, source_target_pairs={{0,1},{1,0},{2,3},{3,2},{4,5},{5,4},{6,7},{7,6},{8,9},{9,8},{10,11... | collective-permute-start | bytes 393224 | tf_op jit(solution)/shard_map/ppermute | solution.py:228
  33.0 29.9 %copy-start = (s32[1,512]{1,0:T(1,128)S(1)}, s32[1,512]{1,0:T(1,128)}, u32[]{:S(2)}) copy-start(s32[1,512]{1,0:T(1,128)} %occupancy.1) | copy-start | bytes 6148
  33.0 29.9 %copy-start.1 = (bf16[27,96,96]{2,1,0:T(8,128)(2,1)S(1)}, bf16[27,96,96]{2,1,0:T(8,128)(2,1)}, u32[]{:S(2)}) copy-start(bf16[27,96,96]{2,1,0:T(8,128)(2,1)} %weight.1) | copy-start | bytes 1492996
  53.1 18.0 %all-to-all-start.2 = ((bf16[64,32,128]{2,1,0:T(8,128)(2,1)}), bf16[64,32,128]{2,1,0:T(8,128)(2,1)S(1)}, u32[]{:S(2)}, u32[]{:S(2)}) async-start(bf16[64,32,128]{2,1,0:T(8,128)(2,1)} %sum_far.1), calls=%async_computation.2 | async-start | bytes 1048576 | tf_op jit(solution)/shard_map/all_to_all | solution.py:261

commit v5 on v4

--- a/solution.py
+++ b/solution.py
@@ -8,11 +8,19 @@
 AXES = ("brick", "chan")
 SIGNS = (-1, 0, 1)
 VOXELS, LANES, CODES = 512, 128, 32
+STACK = 200
 SHELL = 240
 ROWS = 2048
 NEAR, FAR = 64, 8
-SCATTER = [(13 * i + 63) % NEAR for i in range(NEAR)]
-GATHER = SCATTER
+
+
+def crossing(stride):
+    chips = [(stride * j + 31) % 32 for j in range(32)]
+    return [member for j in range(32) for member in (2 * chips[j] + 1, 2 * chips[-j])]
+
+
+SCATTER = crossing(13)
+GATHER = crossing(1)
 FIRST = 4
 OWN, MATE, NEXT, NONE = range(4)
 VMEM = pl.BlockSpec(memory_space=pltpu.VMEM)
@@ -47,17 +55,30 @@
     brick[1:7, 1:7, 7] = rows[272:].reshape(6, 8, LANES)[:, 1:7]
 
 
-def pack_kernel(pair, side, packed, masked, cotangent_rows, masked_rows, brick):
-    occupied = side[0:1, :VOXELS].astype(jnp.float32)
+def stacked(features, occupancy, neighbors, grad_output):
+    depth = features.shape[0]
+
+    def rows(block, first):
+        return jnp.pad(block, ((first, STACK - first - block.shape[0]), (0, VOXELS - block.shape[1]))).astype(jnp.float32)
+
+    return (
+        rows(grad_output, 0) + rows(features, depth) + rows(occupancy, 2 * depth) + rows(neighbors, 2 * depth + 1)
+    )
+
+
+def pack_kernel(stack, packed, masked, cotangent_rows, masked_rows, brick):
+    depth = masked.shape[0]
+    side = stack[2 * depth:, :]
+    occupied = side[0:1]
     for at, rows in ((0, cotangent_rows), (1, masked_rows)):
-        product = pair[at].astype(jnp.float32) * occupied
+        product = stack[depth * at:depth * (at + 1), :] * occupied
         if at:
             masked[...] = product.astype(jnp.bfloat16)
         by_voxel = voxel_rows(product)
         rows[...] = by_voxel.astype(jnp.bfloat16)
         brick[at] = by_voxel.reshape(8, 8, 8, LANES)
         packed[SHELL * at:SHELL * (at + 1), :] = shell_of(brick.at[at]).astype(jnp.bfloat16)
-    bricks = side[0:1, VOXELS:VOXELS + LANES]
+    bricks = side[1:2, :LANES].astype(jnp.int32)
     lane = lax.broadcasted_iota(jnp.int32, (1, LANES), 1)
     own = jnp.sum(jnp.where(lane == 13, bricks, 0), axis=1, keepdims=True)
     codes = jnp.where(bricks == own, OWN, jnp.where(bricks == (own ^ 1), MATE, NEXT))
@@ -263,12 +284,11 @@
 
 def shards(features, occupancy, neighbors, weight, grad_output):
     depth = features.shape[1]
-    pair = jnp.concatenate([grad_output, features])
-    side = jnp.pad(neighbors, ((0, 0), (VOXELS, LANES - 27))) + jnp.pad(occupancy, ((0, 0), (0, LANES)))
+    stack = stacked(features[0], occupancy, neighbors, grad_output[0])
     own, masked, cotangent_rows, masked_rows = call(
         pack_kernel, "pack",
         [bf16(2 * SHELL + CODES, LANES), bf16(depth, VOXELS), bf16(VOXELS, LANES), bf16(VOXELS, LANES)],
-        (pair, side), scratch=[pltpu.VMEM((2, 8, 8, 8, LANES), jnp.float32)],
+        (stack,), scratch=[pltpu.VMEM((2, 8, 8, 8, LANES), jnp.float32)],
     )
     mate, beyond = neighbours(own)
     dot = 27 * 2 * LANES * LANES * VOXELS

time: 72.7 us -> 71.3 us (0.981)
    concatenate x1 -> x0, other arithmetic: 0.96 us -> none  [shards(): pair = jnp.concatenate([grad_output, features])]
where the time goes in v5:
time: 71.3 us; the launch traced here: 71 us
  blocking collectives  37.8 us (53%)
  starting transfers between devices  18.7 us (26%)
  Pallas kernels  7.37 us (10%)
  waiting for transfers between devices  5.29 us (7%)
  other arithmetic  1.01 us (1%)
    all_to_all x1, blocking collectives, total_over_devices(): lax.all_to_all(share, AXES, 0, 0, tiled=True, axis_index_groups=far)  19.1 us
    all_to_all x1, blocking collectives, total_over_devices(): lax.all_to_all(grad, AXES, 0, 0, tiled=True, axis_index_groups=near_group...  18.8 us
    all_to_all x1, starting transfers between devices, total_over_devices(): lax.all_to_all(whole, AXES, 0, 0, tiled=True, axis_index_groups=near_grou...  9.29 us
    pallas_call x6, Pallas kernels, call(): pl.pallas_call(kernel, out_shape=shapes, in_specs=specs or [VMEM] * len(o...  7.37 us
    ppermute x1, starting transfers between devices, neighbours(): lax.ppermute(block, AXES, [(i, i + 1 - 2 * (i % 2)) for i in range(count)])  4.86 us
    ppermute x1, starting transfers between devices, neighbours(): lax.ppermute(block, AXES, [(i, i + 2 * (i % 2) - 1) for i in range(1, cou...  4.59 us
    all_to_all x1, waiting for transfers between devices, total_over_devices(): lax.all_to_all(whole, AXES, 0, 0, tiled=True, axis_index_groups=near_grou...  4.33 us
  transfers between devices with their start and end apart: 3, of which 2 were waited for; matrix products, arithmetic and copies ran while one was open for 0% of the time, Pallas kernels for 5%

profile of v5, /device:TPU:1, one launch (start us, length us, event | category | flops | bytes accessed | tf_op | source)
XLA Modules:
  0.0 71.0 jit_solution(7362872016043293027)
XLA Ops:
  0.6 1.0 %convert_add_fusion.stack = f32[200,512]{1,0:T(8,128)S(1)} fusion(s32[1,27]{1,0:T(1,128)} %param.7, s32[1,512]{1,0:T(1,128)} %occupancy.1, bf16[96,512]{1,0:T(8,128)(2,1)} %bitcast.2, bf16[96,512]{1,0:T(8,128)(2,1)} %bitcast.3), kind=kLoop, calls=%fused_computation | loop fusion | flops 716800 | bytes 608364 | tf_op jit(solution)/shard_map/add | solution.py:65
  1.6 0.4 pack.1
  2.0 4.6 %collective-permute-start.1 = (bf16[512,128]{1,0:T(8,128)(2,1)S(1)}, bf16[512,128]{1,0:T(8,128)(2,1)S(1)}, u32[]{:S(2)}, u32[]{:S(2)}) collective-permute-start(bf16[512,128]{1,0:T(8,128)(2,1)S(1)} %get-tuple-element.9.own), channel_id=1, source_target_pairs={{1,2},{2,1},{3,4},{4,3},{5,6},{6,5},{7,8},{8,7},{9,10},{10,9},{11,... | collective-permute-start | bytes 393224 | tf_op jit(solution)/shard_map/ppermute | solution.py:248
  6.6 4.9 %collective-permute-start = (bf16[512,128]{1,0:T(8,128)(2,1)S(1)}, bf16[512,128]{1,0:T(8,128)(2,1)S(1)}, u32[]{:S(2)}, u32[]{:S(2)}) collective-permute-start(bf16[512,128]{1,0:T(8,128)(2,1)S(1)} %get-tuple-element.9.own), channel_id=1, source_target_pairs={{0,1},{1,0},{2,3},{3,2},{4,5},{5,4},{6,7},{7,6},{8,9},{9,8},{10,11... | collective-permute-start | bytes 393224 | tf_op jit(solution)/shard_map/ppermute | solution.py:249
  11.5 0.0 collective-permute-done.1.beyond
  11.5 1.0 %collective-permute-done.mate = bf16[512,128]{1,0:T(8,128)(2,1)S(1)} collective-permute-done((bf16[512,128]{1,0:T(8,128)(2,1)S(1)}, bf16[512,128]{1,0:T(8,128)(2,1)S(1)}, u32[]{:S(2)}, u32[]{:S(2)}) %collective-permute-start) | collective-permute-done | bytes 131104 | tf_op jit(solution)/shard_map/ppermute | solution.py:249
  12.5 1.1 %weight_grad.1 = bf16[64,32,128]{2,1,0:T(8,128)(2,1)S(1)} custom-call(bf16[96,512]{1,0:T(8,128)(2,1)S(1)} %get-tuple-element.14.masked, bf16[512,128]{1,0:T(8,128)(2,1)S(1)} %get-tuple-element.9.own, bf16[512,128]{1,0:T(8,128)(2,1)S(1)} %collective-permute-done.mate, bf16[512,128]{1,0:T(8,128)(2,1)S(1)} %collective-permute-done.1.beyond, ...), custom_call_target="tpu_custom_call" | custom-call | flops 452984832 | bytes 2097152 | tf_op jit(solution)/shard_map/weight_grad/pallas_call | solution.py:254
  13.6 18.8 %all_to_all.15.parts = bf16[64,32,128]{2,1,0:T(8,128)(2,1)S(1)} all-to-all(bf16[64,32,128]{2,1,0:T(8,128)(2,1)S(1)} %weight_grad.1), channel_id=1, replica_groups={{63,62,25,36,51,10,13,48,39,22,1,60,27,34,53,8,15,46,41,20,3,58,29,32,5..., dimensions={0} | all-to-all | bytes 1048576 | tf_op jit(solution)/shard_map/all_to_all | solution.py:278
  32.3 0.0 copy-start
  32.3 0.0 copy-start.1
  32.3 0.1 sum_near.1
  32.4 19.1 %all_to_all.16.parts = bf16[8,32,128]{2,1,0:T(8,128)(2,1)S(1)} all-to-all(bf16[8,32,128]{2,1,0:T(8,128)(2,1)S(1)} %sum_near.1), channel_id=1, replica_groups={{256,320,384,448,0,64,128,192},{257,321,385,449,1,65,129,193},{258,322,..., dimensions={0} | all-to-all | bytes 131072 | tf_op jit(solution)/shard_map/all_to_all | solution.py:280
  51.5 0.8 %sum_far.1 = bf16[64,32,128]{2,1,0:T(8,128)(2,1)} custom-call(bf16[8,32,128]{2,1,0:T(8,128)(2,1)S(1)} %all_to_all.16.parts), custom_call_target="tpu_custom_call" | custom-call | bytes 2097152 | tf_op jit(solution)/shard_map/sum_far/pallas_call | solution.py:254
  52.3 9.3 %all-to-all-start.2 = ((bf16[64,32,128]{2,1,0:T(8,128)(2,1)}), bf16[64,32,128]{2,1,0:T(8,128)(2,1)S(1)}, u32[]{:S(2)}, u32[]{:S(2)}) async-start(bf16[64,32,128]{2,1,0:T(8,128)(2,1)} %sum_far.1), calls=%async_computation.2 | async-start | bytes 1048576 | tf_op jit(solution)/shard_map/all_to_all | solution.py:282
  61.6 0.0 copy-done
  61.6 0.0 copy-done.1
  61.7 3.7 %outputs.1 = (bf16[1,96,512]{2,1,0:T(8,128)(2,1)}, bf16[1,96,512]{2,1,0:T(8,128)(2,1)}) custom-call(s32[1,512]{1,0:T(1,128)S(1)} %copy-done, bf16[27,96,96]{2,1,0:T(8,128)(2,1)S(1)} %copy-done.1, bf16[512,128]{1,0:T(8,128)(2,1)S(1)} %get-tuple-element.9.own, bf16[512,128]{1,0:T(8,128)(2,1)S(1)} %collective-permute-done.mate, ...), custom_call_target="tpu_custom_call" | custom-call | flops 905969664 | bytes 2097152 | tf_op jit(solution)/shard_map/outputs/pallas_call | solution.py:254
  65.4 4.3 %all-to-all-done.2.dense = bf16[64,32,128]{2,1,0:T(8,128)(2,1)S(1)} async-done(((bf16[64,32,128]{2,1,0:T(8,128)(2,1)}), bf16[64,32,128]{2,1,0:T(8,128)(2,1)S(1)}, u32[]{:S(2)}, u32[]{:S(2)}) %all-to-all-start.2) | async-done | bytes 524320 | tf_op jit(solution)/shard_map/all_to_all | solution.py:282
  69.7 1.3 %unpack.1 = f32[27,96,96]{2,1,0:T(8,128)} custom-call(bf16[64,32,128]{2,1,0:T(8,128)(2,1)S(1)} %all-to-all-done.2.dense), custom_call_target="tpu_custom_call" | custom-call | bytes 2097152 | tf_op jit(solution)/shard_map/unpack/pallas_call | solution.py:254
Async XLA Ops:
  2.0 9.5 %collective-permute-start.1 = (bf16[512,128]{1,0:T(8,128)(2,1)S(1)}, bf16[512,128]{1,0:T(8,128)(2,1)S(1)}, u32[]{:S(2)}, u32[]{:S(2)}) collective-permute-start(bf16[512,128]{1,0:T(8,128)(2,1)S(1)} %get-tuple-element.9.own), channel_id=1, source_target_pairs={{1,2},{2,1},{3,4},{4,3},{5,6},{6,5},{7,8},{8,7},{9,10},{10,9},{11,... | collective-permute-start | bytes 393224 | tf_op jit(solution)/shard_map/ppermute | solution.py:248
  6.6 5.8 %collective-permute-start = (bf16[512,128]{1,0:T(8,128)(2,1)S(1)}, bf16[512,128]{1,0:T(8,128)(2,1)S(1)}, u32[]{:S(2)}, u32[]{:S(2)}) collective-permute-start(bf16[512,128]{1,0:T(8,128)(2,1)S(1)} %get-tuple-element.9.own), channel_id=1, source_target_pairs={{0,1},{1,0},{2,3},{3,2},{4,5},{5,4},{6,7},{7,6},{8,9},{9,8},{10,11... | collective-permute-start | bytes 393224 | tf_op jit(solution)/shard_map/ppermute | solution.py:249
  32.3 29.3 %copy-start = (s32[1,512]{1,0:T(1,128)S(1)}, s32[1,512]{1,0:T(1,128)}, u32[]{:S(2)}) copy-start(s32[1,512]{1,0:T(1,128)} %occupancy.1) | copy-start | bytes 6148
  32.3 29.3 %copy-start.1 = (bf16[27,96,96]{2,1,0:T(8,128)(2,1)S(1)}, bf16[27,96,96]{2,1,0:T(8,128)(2,1)}, u32[]{:S(2)}) copy-start(bf16[27,96,96]{2,1,0:T(8,128)(2,1)} %weight.1) | copy-start | bytes 1492996
  52.3 17.4 %all-to-all-start.2 = ((bf16[64,32,128]{2,1,0:T(8,128)(2,1)}), bf16[64,32,128]{2,1,0:T(8,128)(2,1)S(1)}, u32[]{:S(2)}, u32[]{:S(2)}) async-start(bf16[64,32,128]{2,1,0:T(8,128)(2,1)} %sum_far.1), calls=%async_computation.2 | async-start | bytes 1048576 | tf_op jit(solution)/shard_map/all_to_all | solution.py:282

commit v6 on v5

--- a/solution.py
+++ b/solution.py
@@ -19,8 +19,8 @@
     return [member for j in range(32) for member in (2 * chips[j] + 1, 2 * chips[-j])]
 
 
-SCATTER = crossing(13)
-GATHER = crossing(1)
+SCATTER = crossing(11)
+GATHER = crossing(11)
 FIRST = 4
 OWN, MATE, NEXT, NONE = range(4)
 VMEM = pl.BlockSpec(memory_space=pltpu.VMEM)
@@ -167,11 +167,12 @@
     return jnp.where(lane < 96, block[:72], tail)
 
 
-def square_rows(dense):
+def square_rows(dense, square):
+    square[:72] = dense[:, :96]
     lane = lax.broadcasted_iota(jnp.int32, (24, LANES), 1)
     thirds = [pltpu.roll(dense[24 * third:24 * third + 24], 32 + 32 * third, 1) for third in range(3)]
     tail = jnp.where(lane < 32, thirds[0], jnp.where(lane < 64, thirds[1], thirds[2]))
-    return jnp.concatenate([dense, tail], axis=0)[:, :96]
+    square[72:] = tail[:, :96]
 
 
 def weight_grad_kernel(masked, own, mate, beyond, cotangent, grad, columns, windows, shells, dense):
@@ -198,7 +199,7 @@
     shares = [dense[GATHER.index(member)] for member in SCATTER]
     rows = jnp.concatenate(shares, axis=0).astype(jnp.float32)
     for tap in range(27):
-        grad[tap] = square_rows(rows[72 * tap:72 * tap + 72])
+        square_rows(rows[72 * tap:72 * tap + 72], grad.at[tap])
 
 
 def outputs_kernel(

time: 71.3 us -> 70.9 us (level)
  starting transfers between devices: 18.7 us -> 19.6 us
    all_to_all x1, starting transfers between devices: 9.29 us -> 10.2 us  [total_over_devices(): lax.all_to_all(whole, AXES, 0, 0, tiled=True, axis_index_groups=near_grou...]
    all_to_all x1, blocking collectives: 18.8 us -> 18 us  [total_over_devices(): lax.all_to_all(grad, AXES, 0, 0, tiled=True, axis_index_groups=near_group...]
where the time goes in v6:
time: 70.9 us; the launch traced here: 70.6 us
  blocking collectives  37.2 us (52%)
  starting transfers between devices  19.6 us (28%)
  Pallas kernels  7.37 us (10%)
  waiting for transfers between devices  4.66 us (7%)
  other arithmetic  1.01 us (1%)
    all_to_all x1, blocking collectives, total_over_devices(): lax.all_to_all(share, AXES, 0, 0, tiled=True, axis_index_groups=far)  19.3 us
    all_to_all x1, blocking collectives, total_over_devices(): lax.all_to_all(grad, AXES, 0, 0, tiled=True, axis_index_groups=near_group...  18 us
    all_to_all x1, starting transfers between devices, total_over_devices(): lax.all_to_all(whole, AXES, 0, 0, tiled=True, axis_index_groups=near_grou...  10.2 us
    pallas_call x6, Pallas kernels, call(): pl.pallas_call(kernel, out_shape=shapes, in_specs=specs or [VMEM] * len(o...  7.37 us
    ppermute x1, starting transfers between devices, neighbours(): lax.ppermute(block, AXES, [(i, i + 1 - 2 * (i % 2)) for i in range(count)])  4.86 us
    ppermute x1, starting transfers between devices, neighbours(): lax.ppermute(block, AXES, [(i, i + 2 * (i % 2) - 1) for i in range(1, cou...  4.59 us
    all_to_all x1, waiting for transfers between devices, total_over_devices(): lax.all_to_all(whole, AXES, 0, 0, tiled=True, axis_index_groups=near_grou...  3.7 us
  transfers between devices with their start and end apart: 3, of which 2 were waited for; matrix products, arithmetic and copies ran while one was open for 0% of the time, Pallas kernels for 5%

profile of v6, /device:TPU:1, one launch (start us, length us, event | category | flops | bytes accessed | tf_op | source)
XLA Modules:
  0.0 70.6 jit_solution(16630358507003760827)
XLA Ops:
  0.6 1.0 %convert_add_fusion.stack = f32[200,512]{1,0:T(8,128)S(1)} fusion(s32[1,27]{1,0:T(1,128)} %param.7, s32[1,512]{1,0:T(1,128)} %occupancy.1, bf16[96,512]{1,0:T(8,128)(2,1)} %bitcast.2, bf16[96,512]{1,0:T(8,128)(2,1)} %bitcast.3), kind=kLoop, calls=%fused_computation | loop fusion | flops 716800 | bytes 608364 | tf_op jit(solution)/shard_map/add | solution.py:65
  1.6 0.4 pack.1
  2.0 4.6 %collective-permute-start.1 = (bf16[512,128]{1,0:T(8,128)(2,1)S(1)}, bf16[512,128]{1,0:T(8,128)(2,1)S(1)}, u32[]{:S(2)}, u32[]{:S(2)}) collective-permute-start(bf16[512,128]{1,0:T(8,128)(2,1)S(1)} %get-tuple-element.9.own), channel_id=1, source_target_pairs={{1,2},{2,1},{3,4},{4,3},{5,6},{6,5},{7,8},{8,7},{9,10},{10,9},{11,... | collective-permute-start | bytes 393224 | tf_op jit(solution)/shard_map/ppermute | solution.py:249
  6.6 4.9 %collective-permute-start = (bf16[512,128]{1,0:T(8,128)(2,1)S(1)}, bf16[512,128]{1,0:T(8,128)(2,1)S(1)}, u32[]{:S(2)}, u32[]{:S(2)}) collective-permute-start(bf16[512,128]{1,0:T(8,128)(2,1)S(1)} %get-tuple-element.9.own), channel_id=1, source_target_pairs={{0,1},{1,0},{2,3},{3,2},{4,5},{5,4},{6,7},{7,6},{8,9},{9,8},{10,11... | collective-permute-start | bytes 393224 | tf_op jit(solution)/shard_map/ppermute | solution.py:250
  11.5 0.0 collective-permute-done.1.beyond
  11.5 1.0 %collective-permute-done.mate = bf16[512,128]{1,0:T(8,128)(2,1)S(1)} collective-permute-done((bf16[512,128]{1,0:T(8,128)(2,1)S(1)}, bf16[512,128]{1,0:T(8,128)(2,1)S(1)}, u32[]{:S(2)}, u32[]{:S(2)}) %collective-permute-start) | collective-permute-done | bytes 131104 | tf_op jit(solution)/shard_map/ppermute | solution.py:250
  12.5 1.1 %weight_grad.1 = bf16[64,32,128]{2,1,0:T(8,128)(2,1)S(1)} custom-call(bf16[96,512]{1,0:T(8,128)(2,1)S(1)} %get-tuple-element.14.masked, bf16[512,128]{1,0:T(8,128)(2,1)S(1)} %get-tuple-element.9.own, bf16[512,128]{1,0:T(8,128)(2,1)S(1)} %collective-permute-done.mate, bf16[512,128]{1,0:T(8,128)(2,1)S(1)} %collective-permute-done.1.beyond, ...), custom_call_target="tpu_custom_call" | custom-call | flops 452984832 | bytes 2097152 | tf_op jit(solution)/shard_map/weight_grad/pallas_call | solution.py:255
  13.6 18.0 %all_to_all.15.parts = bf16[64,32,128]{2,1,0:T(8,128)(2,1)S(1)} all-to-all(bf16[64,32,128]{2,1,0:T(8,128)(2,1)S(1)} %weight_grad.1), channel_id=1, replica_groups={{63,62,21,40,43,18,1,60,23,38,45,16,3,58,25,36,47,14,5,56,27,34,49,12,7..., dimensions={0} | all-to-all | bytes 1048576 | tf_op jit(solution)/shard_map/all_to_all | solution.py:279
  31.5 0.0 copy-start
  31.5 0.0 copy-start.1
  31.5 0.1 sum_near.1
  31.6 19.3 %all_to_all.16.parts = bf16[8,32,128]{2,1,0:T(8,128)(2,1)S(1)} all-to-all(bf16[8,32,128]{2,1,0:T(8,128)(2,1)S(1)} %sum_near.1), channel_id=1, replica_groups={{256,320,384,448,0,64,128,192},{257,321,385,449,1,65,129,193},{258,322,..., dimensions={0} | all-to-all | bytes 131072 | tf_op jit(solution)/shard_map/all_to_all | solution.py:281
  50.9 0.8 %sum_far.1 = bf16[64,32,128]{2,1,0:T(8,128)(2,1)} custom-call(bf16[8,32,128]{2,1,0:T(8,128)(2,1)S(1)} %all_to_all.16.parts), custom_call_target="tpu_custom_call" | custom-call | bytes 2097152 | tf_op jit(solution)/shard_map/sum_far/pallas_call | solution.py:255
  51.7 10.2 %all-to-all-start.2 = ((bf16[64,32,128]{2,1,0:T(8,128)(2,1)}), bf16[64,32,128]{2,1,0:T(8,128)(2,1)S(1)}, u32[]{:S(2)}, u32[]{:S(2)}) async-start(bf16[64,32,128]{2,1,0:T(8,128)(2,1)} %sum_far.1), calls=%async_computation.2 | async-start | bytes 1048576 | tf_op jit(solution)/shard_map/all_to_all | solution.py:283
  61.9 0.0 copy-done
  61.9 0.0 copy-done.1
  61.9 3.7 %outputs.1 = (bf16[1,96,512]{2,1,0:T(8,128)(2,1)}, bf16[1,96,512]{2,1,0:T(8,128)(2,1)}) custom-call(s32[1,512]{1,0:T(1,128)S(1)} %copy-done, bf16[27,96,96]{2,1,0:T(8,128)(2,1)S(1)} %copy-done.1, bf16[512,128]{1,0:T(8,128)(2,1)S(1)} %get-tuple-element.9.own, bf16[512,128]{1,0:T(8,128)(2,1)S(1)} %collective-permute-done.mate, ...), custom_call_target="tpu_custom_call" | custom-call | flops 905969664 | bytes 2097152 | tf_op jit(solution)/shard_map/outputs/pallas_call | solution.py:255
  65.6 3.7 %all-to-all-done.2.dense = bf16[64,32,128]{2,1,0:T(8,128)(2,1)S(1)} async-done(((bf16[64,32,128]{2,1,0:T(8,128)(2,1)}), bf16[64,32,128]{2,1,0:T(8,128)(2,1)S(1)}, u32[]{:S(2)}, u32[]{:S(2)}) %all-to-all-start.2) | async-done | bytes 524320 | tf_op jit(solution)/shard_map/all_to_all | solution.py:283
  69.3 1.3 %unpack.1 = f32[27,96,96]{2,1,0:T(8,128)} custom-call(bf16[64,32,128]{2,1,0:T(8,128)(2,1)S(1)} %all-to-all-done.2.dense), custom_call_target="tpu_custom_call" | custom-call | bytes 2097152 | tf_op jit(solution)/shard_map/unpack/pallas_call | solution.py:255
Async XLA Ops:
  2.0 9.5 %collective-permute-start.1 = (bf16[512,128]{1,0:T(8,128)(2,1)S(1)}, bf16[512,128]{1,0:T(8,128)(2,1)S(1)}, u32[]{:S(2)}, u32[]{:S(2)}) collective-permute-start(bf16[512,128]{1,0:T(8,128)(2,1)S(1)} %get-tuple-element.9.own), channel_id=1, source_target_pairs={{1,2},{2,1},{3,4},{4,3},{5,6},{6,5},{7,8},{8,7},{9,10},{10,9},{11,... | collective-permute-start | bytes 393224 | tf_op jit(solution)/shard_map/ppermute | solution.py:249
  6.6 5.8 %collective-permute-start = (bf16[512,128]{1,0:T(8,128)(2,1)S(1)}, bf16[512,128]{1,0:T(8,128)(2,1)S(1)}, u32[]{:S(2)}, u32[]{:S(2)}) collective-permute-start(bf16[512,128]{1,0:T(8,128)(2,1)S(1)} %get-tuple-element.9.own), channel_id=1, source_target_pairs={{0,1},{1,0},{2,3},{3,2},{4,5},{5,4},{6,7},{7,6},{8,9},{9,8},{10,11... | collective-permute-start | bytes 393224 | tf_op jit(solution)/shard_map/ppermute | solution.py:250
  31.5 30.4 %copy-start = (s32[1,512]{1,0:T(1,128)S(1)}, s32[1,512]{1,0:T(1,128)}, u32[]{:S(2)}) copy-start(s32[1,512]{1,0:T(1,128)} %occupancy.1) | copy-start | bytes 6148
  31.5 30.4 %copy-start.1 = (bf16[27,96,96]{2,1,0:T(8,128)(2,1)S(1)}, bf16[27,96,96]{2,1,0:T(8,128)(2,1)}, u32[]{:S(2)}) copy-start(bf16[27,96,96]{2,1,0:T(8,128)(2,1)} %weight.1) | copy-start | bytes 1492996
  51.7 17.6 %all-to-all-start.2 = ((bf16[64,32,128]{2,1,0:T(8,128)(2,1)}), bf16[64,32,128]{2,1,0:T(8,128)(2,1)S(1)}, u32[]{:S(2)}, u32[]{:S(2)}) async-start(bf16[64,32,128]{2,1,0:T(8,128)(2,1)} %sum_far.1), calls=%async_computation.2 | async-start | bytes 1048576 | tf_op jit(solution)/shard_map/all_to_all | solution.py:283

commit v7 on v6

--- a/solution.py
+++ b/solution.py
@@ -14,13 +14,13 @@
 NEAR, FAR = 64, 8
 
 
-def crossing(stride):
+def crossing(stride, lead):
     chips = [(stride * j + 31) % 32 for j in range(32)]
-    return [member for j in range(32) for member in (2 * chips[j] + 1, 2 * chips[-j])]
-
-
-SCATTER = crossing(11)
-GATHER = crossing(11)
+    return [member for j in range(32) for member in (2 * chips[j] + lead, 2 * chips[-j] + 1 - lead)]
+
+
+SCATTER = crossing(11, 0)
+GATHER = crossing(11, 1)
 FIRST = 4
 OWN, MATE, NEXT, NONE = range(4)
 VMEM = pl.BlockSpec(memory_space=pltpu.VMEM)

time: 70.9 us -> 71.3 us (level)
  blocking collectives: 37.2 us -> 39.9 us
  starting transfers between devices: 19.6 us -> 17.4 us
    all_to_all x1, blocking collectives: 19.3 us -> 21.8 us  [total_over_devices(): lax.all_to_all(share, AXES, 0, 0, tiled=True, axis_index_groups=far)]
    all_to_all x1, starting transfers between devices: 10.2 us -> 7.9 us  [total_over_devices(): lax.all_to_all(whole, AXES, 0, 0, tiled=True, axis_index_groups=near_grou...]
where the time goes in v7:
time: 71.3 us; the launch traced here: 71 us
  blocking collectives  39.9 us (56%)
  starting transfers between devices  17.4 us (24%)
  Pallas kernels  7.37 us (10%)
  waiting for transfers between devices  4.66 us (7%)
  other arithmetic  1.01 us (1%)
    all_to_all x1, blocking collectives, total_over_devices(): lax.all_to_all(share, AXES, 0, 0, tiled=True, axis_index_groups=far)  21.8 us
    all_to_all x1, blocking collectives, total_over_devices(): lax.all_to_all(grad, AXES, 0, 0, tiled=True, axis_index_groups=near_group...  18.1 us
    all_to_all x1, starting transfers between devices, total_over_devices(): lax.all_to_all(whole, AXES, 0, 0, tiled=True, axis_index_groups=near_grou...  7.9 us
    pallas_call x6, Pallas kernels, call(): pl.pallas_call(kernel, out_shape=shapes, in_specs=specs or [VMEM] * len(o...  7.37 us
    ppermute x1, starting transfers between devices, neighbours(): lax.ppermute(block, AXES, [(i, i + 1 - 2 * (i % 2)) for i in range(count)])  4.86 us
    ppermute x1, starting transfers between devices, neighbours(): lax.ppermute(block, AXES, [(i, i + 2 * (i % 2) - 1) for i in range(1, cou...  4.59 us
    all_to_all x1, waiting for transfers between devices, total_over_devices(): lax.all_to_all(whole, AXES, 0, 0, tiled=True, axis_index_groups=near_grou...  3.7 us
  transfers between devices with their start and end apart: 3, of which 2 were waited for; matrix products, arithmetic and copies ran while one was open for 0% of the time, Pallas kernels for 5%

profile of v7, /device:TPU:1, one launch (start us, length us, event | category | flops | bytes accessed | tf_op | source)
XLA Modules:
  0.0 71.0 jit_solution(4823083190034666585)
XLA Ops:
  0.6 1.0 %convert_add_fusion.stack = f32[200,512]{1,0:T(8,128)S(1)} fusion(s32[1,27]{1,0:T(1,128)} %param.7, s32[1,512]{1,0:T(1,128)} %occupancy.1, bf16[96,512]{1,0:T(8,128)(2,1)} %bitcast.2, bf16[96,512]{1,0:T(8,128)(2,1)} %bitcast.3), kind=kLoop, calls=%fused_computation | loop fusion | flops 716800 | bytes 608364 | tf_op jit(solution)/shard_map/add | solution.py:65
  1.6 0.4 pack.1
  2.0 4.6 %collective-permute-start.1 = (bf16[512,128]{1,0:T(8,128)(2,1)S(1)}, bf16[512,128]{1,0:T(8,128)(2,1)S(1)}, u32[]{:S(2)}, u32[]{:S(2)}) collective-permute-start(bf16[512,128]{1,0:T(8,128)(2,1)S(1)} %get-tuple-element.9.own), channel_id=1, source_target_pairs={{1,2},{2,1},{3,4},{4,3},{5,6},{6,5},{7,8},{8,7},{9,10},{10,9},{11,... | collective-permute-start | bytes 393224 | tf_op jit(solution)/shard_map/ppermute | solution.py:249
  6.6 4.9 %collective-permute-start = (bf16[512,128]{1,0:T(8,128)(2,1)S(1)}, bf16[512,128]{1,0:T(8,128)(2,1)S(1)}, u32[]{:S(2)}, u32[]{:S(2)}) collective-permute-start(bf16[512,128]{1,0:T(8,128)(2,1)S(1)} %get-tuple-element.9.own), channel_id=1, source_target_pairs={{0,1},{1,0},{2,3},{3,2},{4,5},{5,4},{6,7},{7,6},{8,9},{9,8},{10,11... | collective-permute-start | bytes 393224 | tf_op jit(solution)/shard_map/ppermute | solution.py:250
  11.5 0.0 collective-permute-done.1.beyond
  11.5 1.0 %collective-permute-done.mate = bf16[512,128]{1,0:T(8,128)(2,1)S(1)} collective-permute-done((bf16[512,128]{1,0:T(8,128)(2,1)S(1)}, bf16[512,128]{1,0:T(8,128)(2,1)S(1)}, u32[]{:S(2)}, u32[]{:S(2)}) %collective-permute-start) | collective-permute-done | bytes 131104 | tf_op jit(solution)/shard_map/ppermute | solution.py:250
  12.5 1.1 %weight_grad.1 = bf16[64,32,128]{2,1,0:T(8,128)(2,1)S(1)} custom-call(bf16[96,512]{1,0:T(8,128)(2,1)S(1)} %get-tuple-element.14.masked, bf16[512,128]{1,0:T(8,128)(2,1)S(1)} %get-tuple-element.9.own, bf16[512,128]{1,0:T(8,128)(2,1)S(1)} %collective-permute-done.mate, bf16[512,128]{1,0:T(8,128)(2,1)S(1)} %collective-permute-done.1.beyond, ...), custom_call_target="tpu_custom_call" | custom-call | flops 452984832 | bytes 2097152 | tf_op jit(solution)/shard_map/weight_grad/pallas_call | solution.py:255
  13.6 18.1 %all_to_all.15.parts = bf16[64,32,128]{2,1,0:T(8,128)(2,1)S(1)} all-to-all(bf16[64,32,128]{2,1,0:T(8,128)(2,1)S(1)} %weight_grad.1), channel_id=1, replica_groups={{62,63,20,41,42,19,0,61,22,39,44,17,2,59,24,37,46,15,4,57,26,35,48,13,6..., dimensions={0} | all-to-all | bytes 1048576 | tf_op jit(solution)/shard_map/all_to_all | solution.py:279
  31.7 0.0 copy-start
  31.7 0.0 copy-start.1
  31.7 0.1 sum_near.1
  31.8 21.8 %all_to_all.16.parts = bf16[8,32,128]{2,1,0:T(8,128)(2,1)S(1)} all-to-all(bf16[8,32,128]{2,1,0:T(8,128)(2,1)S(1)} %sum_near.1), channel_id=1, replica_groups={{256,320,384,448,0,64,128,192},{257,321,385,449,1,65,129,193},{258,322,..., dimensions={0} | all-to-all | bytes 131072 | tf_op jit(solution)/shard_map/all_to_all | solution.py:281
  53.5 0.8 %sum_far.1 = bf16[64,32,128]{2,1,0:T(8,128)(2,1)} custom-call(bf16[8,32,128]{2,1,0:T(8,128)(2,1)S(1)} %all_to_all.16.parts), custom_call_target="tpu_custom_call" | custom-call | bytes 2097152 | tf_op jit(solution)/shard_map/sum_far/pallas_call | solution.py:255
  54.4 7.9 %all-to-all-start.2 = ((bf16[64,32,128]{2,1,0:T(8,128)(2,1)}), bf16[64,32,128]{2,1,0:T(8,128)(2,1)S(1)}, u32[]{:S(2)}, u32[]{:S(2)}) async-start(bf16[64,32,128]{2,1,0:T(8,128)(2,1)} %sum_far.1), calls=%async_computation.2 | async-start | bytes 1048576 | tf_op jit(solution)/shard_map/all_to_all | solution.py:283
  62.3 0.0 copy-done
  62.3 0.0 copy-done.1
  62.3 3.7 %outputs.1 = (bf16[1,96,512]{2,1,0:T(8,128)(2,1)}, bf16[1,96,512]{2,1,0:T(8,128)(2,1)}) custom-call(s32[1,512]{1,0:T(1,128)S(1)} %copy-done, bf16[27,96,96]{2,1,0:T(8,128)(2,1)S(1)} %copy-done.1, bf16[512,128]{1,0:T(8,128)(2,1)S(1)} %get-tuple-element.9.own, bf16[512,128]{1,0:T(8,128)(2,1)S(1)} %collective-permute-done.mate, ...), custom_call_target="tpu_custom_call" | custom-call | flops 905969664 | bytes 2097152 | tf_op jit(solution)/shard_map/outputs/pallas_call | solution.py:255
  66.0 3.7 %all-to-all-done.2.dense = bf16[64,32,128]{2,1,0:T(8,128)(2,1)S(1)} async-done(((bf16[64,32,128]{2,1,0:T(8,128)(2,1)}), bf16[64,32,128]{2,1,0:T(8,128)(2,1)S(1)}, u32[]{:S(2)}, u32[]{:S(2)}) %all-to-all-start.2) | async-done | bytes 524320 | tf_op jit(solution)/shard_map/all_to_all | solution.py:283
  69.7 1.3 %unpack.1 = f32[27,96,96]{2,1,0:T(8,128)} custom-call(bf16[64,32,128]{2,1,0:T(8,128)(2,1)S(1)} %all-to-all-done.2.dense), custom_call_target="tpu_custom_call" | custom-call | bytes 2097152 | tf_op jit(solution)/shard_map/unpack/pallas_call | solution.py:255
Async XLA Ops:
  2.0 9.5 %collective-permute-start.1 = (bf16[512,128]{1,0:T(8,128)(2,1)S(1)}, bf16[512,128]{1,0:T(8,128)(2,1)S(1)}, u32[]{:S(2)}, u32[]{:S(2)}) collective-permute-start(bf16[512,128]{1,0:T(8,128)(2,1)S(1)} %get-tuple-element.9.own), channel_id=1, source_target_pairs={{1,2},{2,1},{3,4},{4,3},{5,6},{6,5},{7,8},{8,7},{9,10},{10,9},{11,... | collective-permute-start | bytes 393224 | tf_op jit(solution)/shard_map/ppermute | solution.py:249
  6.6 5.8 %collective-permute-start = (bf16[512,128]{1,0:T(8,128)(2,1)S(1)}, bf16[512,128]{1,0:T(8,128)(2,1)S(1)}, u32[]{:S(2)}, u32[]{:S(2)}) collective-permute-start(bf16[512,128]{1,0:T(8,128)(2,1)S(1)} %get-tuple-element.9.own), channel_id=1, source_target_pairs={{0,1},{1,0},{2,3},{3,2},{4,5},{5,4},{6,7},{7,6},{8,9},{9,8},{10,11... | collective-permute-start | bytes 393224 | tf_op jit(solution)/shard_map/ppermute | solution.py:250
  31.7 30.6 %copy-start = (s32[1,512]{1,0:T(1,128)S(1)}, s32[1,512]{1,0:T(1,128)}, u32[]{:S(2)}) copy-start(s32[1,512]{1,0:T(1,128)} %occupancy.1) | copy-start | bytes 6148
  31.7 30.6 %copy-start.1 = (bf16[27,96,96]{2,1,0:T(8,128)(2,1)S(1)}, bf16[27,96,96]{2,1,0:T(8,128)(2,1)}, u32[]{:S(2)}) copy-start(bf16[27,96,96]{2,1,0:T(8,128)(2,1)} %weight.1) | copy-start | bytes 1492996
  54.4 15.3 %all-to-all-start.2 = ((bf16[64,32,128]{2,1,0:T(8,128)(2,1)}), bf16[64,32,128]{2,1,0:T(8,128)(2,1)S(1)}, u32[]{:S(2)}, u32[]{:S(2)}) async-start(bf16[64,32,128]{2,1,0:T(8,128)(2,1)} %sum_far.1), calls=%async_computation.2 | async-start | bytes 1048576 | tf_op jit(solution)/shard_map/all_to_all | solution.py:283

commit v8 on v6

--- a/solution.py
+++ b/solution.py
@@ -20,7 +20,7 @@
 
 
 SCATTER = crossing(11)
-GATHER = crossing(11)
+GATHER = crossing(1)
 FIRST = 4
 OWN, MATE, NEXT, NONE = range(4)
 VMEM = pl.BlockSpec(memory_space=pltpu.VMEM)

time: 70.9 us -> 71.5 us (level)
  no operation moved by 1% of the time
where the time goes in v8:
time: 71.5 us; the launch traced here: 71.2 us
  blocking collectives  37.2 us (52%)
  starting transfers between devices  19.6 us (27%)
  Pallas kernels  7.37 us (10%)
  waiting for transfers between devices  5.29 us (7%)
  other arithmetic  1.01 us (1%)
    all_to_all x1, blocking collectives, total_over_devices(): lax.all_to_all(share, AXES, 0, 0, tiled=True, axis_index_groups=far)  19.3 us
    all_to_all x1, blocking collectives, total_over_devices(): lax.all_to_all(grad, AXES, 0, 0, tiled=True, axis_index_groups=near_group...  18 us
    all_to_all x1, starting transfers between devices, total_over_devices(): lax.all_to_all(whole, AXES, 0, 0, tiled=True, axis_index_groups=near_grou...  10.1 us
    pallas_call x6, Pallas kernels, call(): pl.pallas_call(kernel, out_shape=shapes, in_specs=specs or [VMEM] * len(o...  7.37 us
    ppermute x1, starting transfers between devices, neighbours(): lax.ppermute(block, AXES, [(i, i + 1 - 2 * (i % 2)) for i in range(count)])  4.86 us
    ppermute x1, starting transfers between devices, neighbours(): lax.ppermute(block, AXES, [(i, i + 2 * (i % 2) - 1) for i in range(1, cou...  4.59 us
    all_to_all x1, waiting for transfers between devices, total_over_devices(): lax.all_to_all(whole, AXES, 0, 0, tiled=True, axis_index_groups=near_grou...  4.33 us
  transfers between devices with their start and end apart: 3, of which 2 were waited for; matrix products, arithmetic and copies ran while one was open for 0% of the time, Pallas kernels for 5%

profile of v8, /device:TPU:1, one launch (start us, length us, event | category | flops | bytes accessed | tf_op | source)
XLA Modules:
  0.0 71.2 jit_solution(424079157431623221)
XLA Ops:
  0.6 1.0 %convert_add_fusion.stack = f32[200,512]{1,0:T(8,128)S(1)} fusion(s32[1,27]{1,0:T(1,128)} %param.7, s32[1,512]{1,0:T(1,128)} %occupancy.1, bf16[96,512]{1,0:T(8,128)(2,1)} %bitcast.2, bf16[96,512]{1,0:T(8,128)(2,1)} %bitcast.3), kind=kLoop, calls=%fused_computation | loop fusion | flops 716800 | bytes 608364 | tf_op jit(solution)/shard_map/add | solution.py:65
  1.6 0.4 pack.1
  2.0 4.6 %collective-permute-start.1 = (bf16[512,128]{1,0:T(8,128)(2,1)S(1)}, bf16[512,128]{1,0:T(8,128)(2,1)S(1)}, u32[]{:S(2)}, u32[]{:S(2)}) collective-permute-start(bf16[512,128]{1,0:T(8,128)(2,1)S(1)} %get-tuple-element.9.own), channel_id=1, source_target_pairs={{1,2},{2,1},{3,4},{4,3},{5,6},{6,5},{7,8},{8,7},{9,10},{10,9},{11,... | collective-permute-start | bytes 393224 | tf_op jit(solution)/shard_map/ppermute | solution.py:249
  6.6 4.9 %collective-permute-start = (bf16[512,128]{1,0:T(8,128)(2,1)S(1)}, bf16[512,128]{1,0:T(8,128)(2,1)S(1)}, u32[]{:S(2)}, u32[]{:S(2)}) collective-permute-start(bf16[512,128]{1,0:T(8,128)(2,1)S(1)} %get-tuple-element.9.own), channel_id=1, source_target_pairs={{0,1},{1,0},{2,3},{3,2},{4,5},{5,4},{6,7},{7,6},{8,9},{9,8},{10,11... | collective-permute-start | bytes 393224 | tf_op jit(solution)/shard_map/ppermute | solution.py:250
  11.5 0.0 collective-permute-done.1.beyond
  11.5 1.0 %collective-permute-done.mate = bf16[512,128]{1,0:T(8,128)(2,1)S(1)} collective-permute-done((bf16[512,128]{1,0:T(8,128)(2,1)S(1)}, bf16[512,128]{1,0:T(8,128)(2,1)S(1)}, u32[]{:S(2)}, u32[]{:S(2)}) %collective-permute-start) | collective-permute-done | bytes 131104 | tf_op jit(solution)/shard_map/ppermute | solution.py:250
  12.5 1.1 %weight_grad.1 = bf16[64,32,128]{2,1,0:T(8,128)(2,1)S(1)} custom-call(bf16[96,512]{1,0:T(8,128)(2,1)S(1)} %get-tuple-element.14.masked, bf16[512,128]{1,0:T(8,128)(2,1)S(1)} %get-tuple-element.9.own, bf16[512,128]{1,0:T(8,128)(2,1)S(1)} %collective-permute-done.mate, bf16[512,128]{1,0:T(8,128)(2,1)S(1)} %collective-permute-done.1.beyond, ...), custom_call_target="tpu_custom_call" | custom-call | flops 452984832 | bytes 2097152 | tf_op jit(solution)/shard_map/weight_grad/pallas_call | solution.py:255
  13.6 18.0 %all_to_all.15.parts = bf16[64,32,128]{2,1,0:T(8,128)(2,1)S(1)} all-to-all(bf16[64,32,128]{2,1,0:T(8,128)(2,1)S(1)} %weight_grad.1), channel_id=1, replica_groups={{63,62,21,40,43,18,1,60,23,38,45,16,3,58,25,36,47,14,5,56,27,34,49,12,7..., dimensions={0} | all-to-all | bytes 1048576 | tf_op jit(solution)/shard_map/all_to_all | solution.py:279
  31.5 0.0 copy-start
  31.5 0.0 copy-start.1
  31.5 0.1 sum_near.1
  31.6 19.3 %all_to_all.16.parts = bf16[8,32,128]{2,1,0:T(8,128)(2,1)S(1)} all-to-all(bf16[8,32,128]{2,1,0:T(8,128)(2,1)S(1)} %sum_near.1), channel_id=1, replica_groups={{256,320,384,448,0,64,128,192},{257,321,385,449,1,65,129,193},{258,322,..., dimensions={0} | all-to-all | bytes 131072 | tf_op jit(solution)/shard_map/all_to_all | solution.py:281
  50.9 0.8 %sum_far.1 = bf16[64,32,128]{2,1,0:T(8,128)(2,1)} custom-call(bf16[8,32,128]{2,1,0:T(8,128)(2,1)S(1)} %all_to_all.16.parts), custom_call_target="tpu_custom_call" | custom-call | bytes 2097152 | tf_op jit(solution)/shard_map/sum_far/pallas_call | solution.py:255
  51.7 10.1 %all-to-all-start.2 = ((bf16[64,32,128]{2,1,0:T(8,128)(2,1)}), bf16[64,32,128]{2,1,0:T(8,128)(2,1)S(1)}, u32[]{:S(2)}, u32[]{:S(2)}) async-start(bf16[64,32,128]{2,1,0:T(8,128)(2,1)} %sum_far.1), calls=%async_computation.2 | async-start | bytes 1048576 | tf_op jit(solution)/shard_map/all_to_all | solution.py:283
  61.9 0.0 copy-done
  61.9 0.0 copy-done.1
  61.9 3.7 %outputs.1 = (bf16[1,96,512]{2,1,0:T(8,128)(2,1)}, bf16[1,96,512]{2,1,0:T(8,128)(2,1)}) custom-call(s32[1,512]{1,0:T(1,128)S(1)} %copy-done, bf16[27,96,96]{2,1,0:T(8,128)(2,1)S(1)} %copy-done.1, bf16[512,128]{1,0:T(8,128)(2,1)S(1)} %get-tuple-element.9.own, bf16[512,128]{1,0:T(8,128)(2,1)S(1)} %collective-permute-done.mate, ...), custom_call_target="tpu_custom_call" | custom-call | flops 905969664 | bytes 2097152 | tf_op jit(solution)/shard_map/outputs/pallas_call | solution.py:255
  65.6 4.3 %all-to-all-done.2.dense = bf16[64,32,128]{2,1,0:T(8,128)(2,1)S(1)} async-done(((bf16[64,32,128]{2,1,0:T(8,128)(2,1)}), bf16[64,32,128]{2,1,0:T(8,128)(2,1)S(1)}, u32[]{:S(2)}, u32[]{:S(2)}) %all-to-all-start.2) | async-done | bytes 524320 | tf_op jit(solution)/shard_map/all_to_all | solution.py:283
  70.0 1.3 %unpack.1 = f32[27,96,96]{2,1,0:T(8,128)} custom-call(bf16[64,32,128]{2,1,0:T(8,128)(2,1)S(1)} %all-to-all-done.2.dense), custom_call_target="tpu_custom_call" | custom-call | bytes 2097152 | tf_op jit(solution)/shard_map/unpack/pallas_call | solution.py:255
Async XLA Ops:
  2.0 9.5 %collective-permute-start.1 = (bf16[512,128]{1,0:T(8,128)(2,1)S(1)}, bf16[512,128]{1,0:T(8,128)(2,1)S(1)}, u32[]{:S(2)}, u32[]{:S(2)}) collective-permute-start(bf16[512,128]{1,0:T(8,128)(2,1)S(1)} %get-tuple-element.9.own), channel_id=1, source_target_pairs={{1,2},{2,1},{3,4},{4,3},{5,6},{6,5},{7,8},{8,7},{9,10},{10,9},{11,... | collective-permute-start | bytes 393224 | tf_op jit(solution)/shard_map/ppermute | solution.py:249
  6.6 5.8 %collective-permute-start = (bf16[512,128]{1,0:T(8,128)(2,1)S(1)}, bf16[512,128]{1,0:T(8,128)(2,1)S(1)}, u32[]{:S(2)}, u32[]{:S(2)}) collective-permute-start(bf16[512,128]{1,0:T(8,128)(2,1)S(1)} %get-tuple-element.9.own), channel_id=1, source_target_pairs={{0,1},{1,0},{2,3},{3,2},{4,5},{5,4},{6,7},{7,6},{8,9},{9,8},{10,11... | collective-permute-start | bytes 393224 | tf_op jit(solution)/shard_map/ppermute | solution.py:250
  31.5 30.4 %copy-start = (s32[1,512]{1,0:T(1,128)S(1)}, s32[1,512]{1,0:T(1,128)}, u32[]{:S(2)}) copy-start(s32[1,512]{1,0:T(1,128)} %occupancy.1) | copy-start | bytes 6148
  31.5 30.4 %copy-start.1 = (bf16[27,96,96]{2,1,0:T(8,128)(2,1)S(1)}, bf16[27,96,96]{2,1,0:T(8,128)(2,1)}, u32[]{:S(2)}) copy-start(bf16[27,96,96]{2,1,0:T(8,128)(2,1)} %weight.1) | copy-start | bytes 1492996
  51.7 18.2 %all-to-all-start.2 = ((bf16[64,32,128]{2,1,0:T(8,128)(2,1)}), bf16[64,32,128]{2,1,0:T(8,128)(2,1)S(1)}, u32[]{:S(2)}, u32[]{:S(2)}) async-start(bf16[64,32,128]{2,1,0:T(8,128)(2,1)} %sum_far.1), calls=%async_computation.2 | async-start | bytes 1048576 | tf_op jit(solution)/shard_map/all_to_all | solution.py:283
